TPU v7x, 256 devices: a whole 4x4x8 slice. The times are simulated.
256 devices in a mesh: section: 4 (over z_lo, core), dp: 4 (over x), mp: 16 (over y, z_hi).
Axes of the slice: x: 4, y: 4, z: 8 (z_hi: 4, z_lo: 2; z = z_hi * 2 + z_lo), core: 2. Of those that a mesh axis runs over, the one named last changes fastest.
Arguments:
- caption_tokens: bfloat16 [16, 64, 4096], P('dp', None, 'mp'), may hold values from -6 to 6
- caption_lengths: int32 [16], P('dp'), may hold values from 1 to 64, as said below
- group_ids: int32 [16], replicated, may hold values from 0 to 3, as said below
- text_gain: float32 [4, 4096], P('section'), may hold values from 0.5 to 1.5
- text_gate: bfloat16 [4, 4096, 14336], P('section', 'dp', 'mp'), may hold values from -0.09375 to 0.09375
- text_up: bfloat16 [4, 4096, 14336], P('section', 'dp', 'mp'), may hold values from -0.09375 to 0.09375
- text_down: bfloat16 [4, 14336, 4096], P('section', 'mp', 'dp'), may hold values from -0.0625 to 0.0625
- text_proj: bfloat16 [4096, 768], P('mp'), may hold values from -0.09375 to 0.09375
- image_patches: bfloat16 [4, 256, 1024], P('dp', 'section'), may hold values from -6 to 6
- image_gain: float32 [1024], replicated, may hold values from 0.5 to 1.5
- image_fc1: bfloat16 [1024, 4096], P(None, 'mp'), may hold values from -0.1875 to 0.1875
- image_fc2: bfloat16 [4096, 1024], P('mp'), may hold values from -0.09375 to 0.09375
- image_proj: bfloat16 [1024, 768], replicated, may hold values from -0.1875 to 0.1875
Outputs:
- loss_mean: float32 [], replicated
- grad_captions: float32 [16, 768], P('dp')
- grad_images: float32 [4, 768], P('dp')
Inputs may be any that keep to these rules, and one draw needn't show every extreme that they name: `caption_lengths`: every caption has at least one token; some caption has exactly 64. `group_ids`: each image index is named by exactly four captions.
All inputs are finite; a program needn't handle non-finite values.
Results may differ from a plain program's by a relative error of at most 0.035.
Values may be sent and summed in bfloat16 or wider, within the bound.
A program may use at most 128 MiB of HBM per device.

v0:
```python
import jax
import jax.numpy as jnp
from jax import lax
from jax.sharding import PartitionSpec as P


def passed_along(shard, axis, by):
    devices = lax.axis_size(axis)
    pairs = [(i, i + by) for i in range(devices) if 0 <= i + by < devices]
    return lax.ppermute(shard, axis, pairs)


def contrast_total(caption_unit, image_unit, group_ids):
    logits = 10.0 * jnp.dot(caption_unit, image_unit.T, precision=lax.Precision.HIGHEST)
    matches = (
        group_ids[:, None] == jnp.arange(image_unit.shape[0], dtype=jnp.int32)[None, :]
    ).astype(jnp.float32)
    expo = jnp.exp(logits)
    forward = jnp.log(jnp.sum(expo, 1)) - jnp.sum(logits * matches, 1)
    backward = jnp.log(jnp.sum(expo, 0)) - jnp.log(jnp.sum(expo * matches, 0))
    total = 0.5 * (jnp.sum(forward) + jnp.sum(backward))
    return (total, 0.5 * (jnp.mean(forward) + jnp.mean(backward)))


def unit_rows(matrix):
    return matrix * lax.rsqrt(jnp.sum(matrix * matrix, -1, keepdims=True) + 1e-06)


def per_device(
    caption_tokens,
    caption_lengths,
    group_ids,
    text_gain,
    text_gate,
    text_up,
    text_down,
    text_proj,
    image_patches,
    image_gain,
    image_fc1,
    image_fc2,
    image_proj,
):
    section_pos = lax.axis_index("section")
    sections = lax.axis_size("section")
    gate_full, up_full, down_full = (
        lax.all_gather(text_gate, "dp", axis=1, tiled=True),
        lax.all_gather(text_up, "dp", axis=1, tiled=True),
        lax.all_gather(text_down, "dp", axis=2, tiled=True),
    )
    gate_full = gate_full[0]
    up_full = up_full[0]
    down_full = down_full[0]
    gain_row = text_gain[0]
    micro, length, shard = caption_tokens.shape
    ticks = micro + sections - 1

    def norm_rows(whole):
        values = whole.astype(jnp.float32)
        return (
            values * lax.rsqrt(jnp.mean(values * values, -1, keepdims=True) + 1e-05) * gain_row
        ).astype(jnp.bfloat16)

    def branch_terms(whole):
        normed = norm_rows(whole)
        gate = jnp.dot(normed, gate_full, preferred_element_type=jnp.float32)
        upper = jnp.dot(normed, up_full, preferred_element_type=jnp.float32)
        inner = (jax.nn.silu(gate) * upper).astype(jnp.bfloat16)
        return jnp.dot(inner, down_full, preferred_element_type=jnp.float32)

    def store(finished, output, moment):
        slot = moment - (sections - 1)
        updated = lax.dynamic_update_index_in_dim(finished, output, jnp.maximum(slot, 0), 0)
        return jnp.where(slot >= 0, updated, finished)

    def first_input(source, moment, arrived):
        fresh = lax.dynamic_index_in_dim(source, jnp.minimum(moment, micro - 1), 0, keepdims=False)
        fresh = jnp.where(moment < micro, fresh, jnp.zeros_like(fresh))
        return jnp.where(section_pos == 0, fresh, arrived)

    full_tokens = lax.all_gather(caption_tokens, "mp", axis=2, tiled=True)

    def advance_full(moment, carry):
        arrived, finished = carry
        incoming = first_input(full_tokens, moment, arrived)
        summed = lax.psum(branch_terms(incoming).astype(jnp.bfloat16), "mp").astype(jnp.float32)
        output = (incoming.astype(jnp.float32) + summed).astype(jnp.bfloat16)
        finished = store(finished, output, moment)
        arrived = passed_along(output, "section", 1)
        return (arrived, finished)

    begin = (jnp.zeros((length, full_tokens.shape[2]), jnp.bfloat16), jnp.zeros_like(full_tokens))
    _, finished = lax.fori_loop(0, ticks, advance_full, begin)
    positions = lax.broadcasted_iota(jnp.int32, (micro, length), 1)
    masked = (positions < caption_lengths[:, None]).astype(jnp.float32)
    pooled = (
        jnp.sum(finished.astype(jnp.float32) * masked[:, :, None], 1)
        / caption_lengths.astype(jnp.float32)[:, None]
    )
    pooled = lax.dynamic_slice_in_dim(pooled, lax.axis_index("mp") * shard, shard, 1)
    last_section = (section_pos == sections - 1).astype(jnp.float32)
    caption_term = (
        jnp.dot(pooled.astype(jnp.bfloat16), text_proj, preferred_element_type=jnp.float32)
        * last_section
    )
    caption_embed = lax.psum(caption_term, ("section", "mp"))
    img_count, patch_part, width_v = image_patches.shape
    values = image_patches.reshape(img_count * patch_part, width_v).astype(jnp.float32)
    vnormed = (
        values * lax.rsqrt(jnp.mean(values * values, -1, keepdims=True) + 1e-05) * image_gain
    ).astype(jnp.bfloat16)
    vinner = jax.nn.gelu(
        jnp.dot(vnormed, image_fc1, preferred_element_type=jnp.float32), approximate=False
    ).astype(jnp.bfloat16)
    partial_out = jnp.dot(vinner, image_fc2, preferred_element_type=jnp.float32)
    summed_rows = lax.psum(partial_out.astype(jnp.bfloat16), "mp").astype(jnp.float32)
    patch_term = jnp.sum((values + summed_rows).reshape(img_count, patch_part, width_v), 1)
    image_total = lax.psum(patch_term, "section")
    image_pooled = (image_total / (patch_part * sections)).astype(jnp.bfloat16)
    image_embed = jnp.dot(image_pooled, image_proj, preferred_element_type=jnp.float32)
    all_captions, all_images = (
        lax.all_gather(caption_embed, "dp", axis=0, tiled=True),
        lax.all_gather(image_embed, "dp", axis=0, tiled=True),
    )
    caption_unit = unit_rows(all_captions)
    image_unit = unit_rows(all_images)

    def wrapped(first, second):
        return contrast_total(first, second, group_ids)

    _, pullback, loss_mean = jax.vjp(wrapped, caption_unit, image_unit, has_aux=True)
    grad_all_captions, grad_all_images = pullback(jnp.ones((), jnp.float32))
    dp_pos = lax.axis_index("dp")
    grad_captions = lax.dynamic_slice_in_dim(grad_all_captions, dp_pos * micro, micro, 0)
    grad_images = lax.dynamic_slice_in_dim(grad_all_images, dp_pos * img_count, img_count, 0)
    return (loss_mean, grad_captions, grad_images)


def solution(mesh):
    return jax.shard_map(
        per_device,
        mesh=mesh,
        in_specs=(
            P("dp", None, "mp"),
            P("dp"),
            P(),
            P("section", None),
            P("section", "dp", "mp"),
            P("section", "dp", "mp"),
            P("section", "mp", "dp"),
            P("mp", None),
            P("dp", "section", None),
            P(),
            P(None, "mp"),
            P("mp", None),
            P(),
        ),
        out_specs=(P(), P("dp", None), P("dp", None)),
        check_vma=False,
    )
```

profile of v0, /device:TPU:1, one launch (start us, length us, event | category | flops | bytes accessed | tf_op | source)
XLA Modules:
  0.0 2122.5 jit_solution(3338496091891877991)
XLA Ops:
  13.8 155.8 %all-reduce.3.cloned.1.call-done = bf16[64,1024]{1,0:T(8,128)(2,1)} async-done(((bf16[64,1024]{1,0:T(8,128)(2,1)}), bf16[64,1024]{1,0:T(8,128)(2,1)}) %all-reduce.3.cloned.1.call-update) | async-done | bytes 131088 | tf_op jit(solution)/shard_map/psum | solution.py:116
  170.6 15.9 psum.37
  186.8 9.3 all-gather.2
  196.2 46.2 %all-gather.8.cloned.1.call-done = bf16[4,64,4096]{2,1,0:T(8,128)(2,1)} async-done(((bf16[4,64,256]{2,1,0:T(8,128)(2,1)}), bf16[4,64,4096]{2,1,0:T(8,128)(2,1)}) %all-gather.8.cloned.1.call-update) | async-done | bytes 2097168 | tf_op jit(solution)/shard_map/all_gather | solution.py:81
  242.5 76.6 %all-gather.10.cloned.1.call-done = bf16[1,4096,896]{2,1,0:T(8,128)(2,1)} async-done(((bf16[1,1024,896]{2,1,0:T(8,128)(2,1)}), bf16[1,4096,896]{2,1,0:T(8,128)(2,1)}) %all-gather.10.cloned.1.call-update) | async-done | bytes 7340048 | tf_op jit(solution)/shard_map/all_gather | solution.py:47
  319.0 79.6 %all-gather.12.cloned.1.call-done = bf16[1,4096,896]{2,1,0:T(8,128)(2,1)} async-done(((bf16[1,1024,896]{2,1,0:T(8,128)(2,1)}), bf16[1,4096,896]{2,1,0:T(8,128)(2,1)}) %all-gather.12.cloned.1.call-update) | async-done | bytes 7340048 | tf_op jit(solution)/shard_map/all_gather | solution.py:48
  398.6 79.6 %all-gather.14.cloned.1.call-done = bf16[1,896,4096]{2,1,0:T(8,128)(2,1)} async-done(((bf16[1,896,1024]{2,1,0:T(8,128)(2,1)}), bf16[1,896,4096]{2,1,0:T(8,128)(2,1)}) %all-gather.14.cloned.1.call-update) | async-done | bytes 7340048 | tf_op jit(solution)/shard_map/all_gather | solution.py:49
  479.9 1342.5 %while.17 = (s32[]{:T(128)}, bf16[64,4096]{1,0:T(8,128)(2,1)S(1)}, bf16[4,64,4096]{2,1,0:T(8,128)(2,1)}, pred[]{:T(512)}, bf16[4,64,4096]{2,1,0:T(8,128)(2,1)}, ...) while((s32[]{:T(128)}, bf16[64,4096]{1,0:T(8,128)(2,1)S(1)}, ...), condition=%wide.region_3.4_spmd, body=%wide.region_0.3_spmd.sunk | while | flops 1414873088 | bytes 33523256 | solution.py:93
  494.7 158.0 %all-reduce.5.cloned.1.call-done = bf16[64,4096]{1,0:T(8,128)(2,1)} async-done(((bf16[64,4096]{1,0:T(8,128)(2,1)}), bf16[64,4096]{1,0:T(8,128)(2,1)}) %all-reduce.5.cloned.1.call-update) | async-done | bytes 524304 | tf_op jit(solution)/shard_map/while/body/eval_jaxpr/psum | solution.py:86
  654.9 13.4 collective-permute-start
  689.1 154.8 %all-reduce.5.cloned.1.call-done = bf16[64,4096]{1,0:T(8,128)(2,1)} async-done(((bf16[64,4096]{1,0:T(8,128)(2,1)}), bf16[64,4096]{1,0:T(8,128)(2,1)}) %all-reduce.5.cloned.1.call-update) | async-done | bytes 524304 | tf_op jit(solution)/shard_map/while/body/eval_jaxpr/psum | solution.py:86
  846.1 13.4 collective-permute-start
  880.3 154.8 %all-reduce.5.cloned.1.call-done = bf16[64,4096]{1,0:T(8,128)(2,1)} async-done(((bf16[64,4096]{1,0:T(8,128)(2,1)}), bf16[64,4096]{1,0:T(8,128)(2,1)}) %all-reduce.5.cloned.1.call-update) | async-done | bytes 524304 | tf_op jit(solution)/shard_map/while/body/eval_jaxpr/psum | solution.py:86
  1037.3 13.4 collective-permute-start
  1071.5 154.8 %all-reduce.5.cloned.1.call-done = bf16[64,4096]{1,0:T(8,128)(2,1)} async-done(((bf16[64,4096]{1,0:T(8,128)(2,1)}), bf16[64,4096]{1,0:T(8,128)(2,1)}) %all-reduce.5.cloned.1.call-update) | async-done | bytes 524304 | tf_op jit(solution)/shard_map/while/body/eval_jaxpr/psum | solution.py:86
  1228.6 13.4 collective-permute-start
  1262.8 155.0 %all-reduce.5.cloned.1.call-done = bf16[64,4096]{1,0:T(8,128)(2,1)} async-done(((bf16[64,4096]{1,0:T(8,128)(2,1)}), bf16[64,4096]{1,0:T(8,128)(2,1)}) %all-reduce.5.cloned.1.call-update) | async-done | bytes 524304 | tf_op jit(solution)/shard_map/while/body/eval_jaxpr/psum | solution.py:86
  1420.1 13.4 collective-permute-start
  1454.3 154.8 %all-reduce.5.cloned.1.call-done = bf16[64,4096]{1,0:T(8,128)(2,1)} async-done(((bf16[64,4096]{1,0:T(8,128)(2,1)}), bf16[64,4096]{1,0:T(8,128)(2,1)}) %all-reduce.5.cloned.1.call-update) | async-done | bytes 524304 | tf_op jit(solution)/shard_map/while/body/eval_jaxpr/psum | solution.py:86
  1611.4 13.4 collective-permute-start
  1645.6 154.9 %all-reduce.5.cloned.1.call-done = bf16[64,4096]{1,0:T(8,128)(2,1)} async-done(((bf16[64,4096]{1,0:T(8,128)(2,1)}), bf16[64,4096]{1,0:T(8,128)(2,1)}) %all-reduce.5.cloned.1.call-update) | async-done | bytes 524304 | tf_op jit(solution)/shard_map/while/body/eval_jaxpr/psum | solution.py:86
  1802.8 13.4 collective-permute-start
  1824.9 275.4 %psum.35 = f32[4,768]{1,0:T(4,128)S(1)} all-reduce(f32[4,768]{1,0:T(4,128)S(1)} %convolution_multiply_fusion.1), channel_id=1, replica_groups=mesh['section'=4,'dp'=4,'mp'=16] {'section','mp'}, use_global_device_ids=true, to_apply=%region_5.6 | all-reduce | flops 3072 | bytes 24576 | tf_op jit(solution)/shard_map/psum | solution.py:106
  2100.2 9.3 all-gather.1
  (101 shorter events, 176.5 us)
Async XLA Ops:
  7.2 179.3 %copy-start = (bf16[1024,768]{1,0:T(8,128)(2,1)S(1)}, bf16[1024,768]{1,0:T(8,128)(2,1)}, u32[]{:S(2)}) copy-start(bf16[1024,768]{1,0:T(8,128)(2,1)} %param.27) | copy-start | bytes 4718596
  7.2 162.5 %all-reduce.3.cloned.1.call-start = ((), (), s32[]{:S(2)}) async-start(), calls=%async_computation.4 | async-start | bytes 262144 | tf_op jit(solution)/shard_map/psum | solution.py:116
  11.0 231.4 %all-gather.8.cloned.1.call-start = ((), (), s32[]{:S(2)}) async-start(), calls=%async_computation | async-start | bytes 2228224 | tf_op jit(solution)/shard_map/all_gather | solution.py:81
  11.8 307.2 %all-gather.10.cloned.1.call-start = ((), (), s32[]{:S(2)}) async-start(), calls=%async_computation.1 | async-start | bytes 9175040 | tf_op jit(solution)/shard_map/all_gather | solution.py:47
  12.5 157.1 %copy-start.2 = (bf16[1,64,1024]{2,1,0:T(8,128)(2,1)S(1)}, bf16[1,64,1024]{2,1,0:T(8,128)(2,1)}, u32[]{:S(2)}) copy-start(bf16[1,64,1024]{2,1,0:T(8,128)(2,1)} %param.23) | copy-start | bytes 393220
  12.5 386.1 %all-gather.12.cloned.1.call-start = ((), (), s32[]{:S(2)}) async-start(), calls=%async_computation.2 | async-start | bytes 9175040 | tf_op jit(solution)/shard_map/all_gather | solution.py:48
  13.1 465.1 %all-gather.14.cloned.1.call-start = ((), (), s32[]{:S(2)}) async-start(), calls=%async_computation.3 | async-start | bytes 9175040 | tf_op jit(solution)/shard_map/all_gather | solution.py:49
  186.5 293.4 %copy-start.1 = (f32[1,4096]{1,0:T(1,128)S(1)}, f32[1,4096]{1,0:T(1,128)}, u32[]{:S(2)}) copy-start(f32[1,4096]{1,0:T(1,128)} %param.18) | copy-start | bytes 49156
  479.9 172.7 %all-reduce.5.cloned.1.call-start = ((), (), s32[]{:S(2)}) async-start(), calls=%async_computation.5 | async-start | bytes 1048576 | tf_op jit(solution)/shard_map/while/body/eval_jaxpr/psum | solution.py:86
  654.9 19.5 collective-permute-start
  674.4 169.5 %all-reduce.5.cloned.1.call-start = ((), (), s32[]{:S(2)}) async-start(), calls=%async_computation.5 | async-start | bytes 1048576 | tf_op jit(solution)/shard_map/while/body/eval_jaxpr/psum | solution.py:86
  846.1 19.5 collective-permute-start
  865.6 169.5 %all-reduce.5.cloned.1.call-start = ((), (), s32[]{:S(2)}) async-start(), calls=%async_computation.5 | async-start | bytes 1048576 | tf_op jit(solution)/shard_map/while/body/eval_jaxpr/psum | solution.py:86
  1037.3 19.5 collective-permute-start
  1056.9 169.5 %all-reduce.5.cloned.1.call-start = ((), (), s32[]{:S(2)}) async-start(), calls=%async_computation.5 | async-start | bytes 1048576 | tf_op jit(solution)/shard_map/while/body/eval_jaxpr/psum | solution.py:86
  1228.6 19.5 collective-permute-start
  1248.1 169.7 %all-reduce.5.cloned.1.call-start = ((), (), s32[]{:S(2)}) async-start(), calls=%async_computation.5 | async-start | bytes 1048576 | tf_op jit(solution)/shard_map/while/body/eval_jaxpr/psum | solution.py:86
  1420.1 19.5 collective-permute-start
  1439.6 169.5 %all-reduce.5.cloned.1.call-start = ((), (), s32[]{:S(2)}) async-start(), calls=%async_computation.5 | async-start | bytes 1048576 | tf_op jit(solution)/shard_map/while/body/eval_jaxpr/psum | solution.py:86
  1611.4 19.5 collective-permute-start
  1630.9 169.6 %all-reduce.5.cloned.1.call-start = ((), (), s32[]{:S(2)}) async-start(), calls=%async_computation.5 | async-start | bytes 1048576 | tf_op jit(solution)/shard_map/while/body/eval_jaxpr/psum | solution.py:86
  1802.8 19.6 collective-permute-start
  1822.4 2.3 copy-start.3
  1822.4 287.3 %copy-start.5 = (s32[16]{0:T(128)S(1)}, s32[16]{0:T(128)}, u32[]{:S(2)}) copy-start(s32[16]{0:T(128)} %param.17) | copy-start | bytes 196
  (1 other events, 1.2 us)
Sparse Core Ops, SparseCore 0:
  11.1 158.4 all-reduce.2
  172.3 70.0 all-gather.7
  244.4 74.5 all-gather.9
  320.8 77.7 all-gather.11
  400.4 77.7 all-gather.13
  494.8 157.7 all-reduce.4
  689.2 154.6 all-reduce.4
  880.4 154.6 all-reduce.4
  1071.7 154.6 all-reduce.4
  1262.9 154.8 all-reduce.4
  1454.4 154.6 all-reduce.4
  1645.7 154.7 all-reduce.4
where the time goes:
time: 2160 us; the launch traced here: 2120 us
  waiting for transfers between devices  1570 us (73%)
  blocking collectives  310 us (14%)
  matrix products  96.8 us (4%)
  starting transfers between devices  94.3 us (4%)
  other arithmetic  31.2 us (1%)
    psum x7, waiting for transfers between devices, advance_full(): lax.psum(branch_terms(incoming).astype(jnp.bfloat16), 'mp')  1090 us
    psum x1, blocking collectives, per_device(): caption_embed = lax.psum(caption_term, ('section', 'mp'))  275 us
    psum x1, waiting for transfers between devices, per_device(): lax.psum(partial_out.astype(jnp.bfloat16), 'mp').astype(jnp.float32)  156 us
    ppermute x7, starting transfers between devices, passed_along(): return lax.ppermute(shard, axis, pairs)  94 us
    all_gather x1, waiting for transfers between devices, per_device(): lax.all_gather(text_up, 'dp', axis=1, tiled=True)  79.6 us
    all_gather x1, waiting for transfers between devices, per_device(): lax.all_gather(text_down, 'dp', axis=2, tiled=True)  79.6 us
    all_gather x1, waiting for transfers between devices, per_device(): lax.all_gather(text_gate, 'dp', axis=1, tiled=True)  76.6 us
    dot_general x7, matrix products, branch_terms(): return jnp.dot(inner, down_full, preferred_element_type=jnp.float32)  61.3 us
  transfers between devices with their start and end apart: 19, of which 19 were waited for; matrix products, arithmetic and copies ran while one was open for 0% of the time, Pallas kernels for 0%

commit v1 on v0

v1 whole, which is shorter than its diff:
```python
import functools

import jax
import jax.numpy as jnp
from jax import lax
from jax.experimental import pallas as pl
from jax.experimental.pallas import tpu as pltpu
from jax.sharding import PartitionSpec as P

MESH = pl.DeviceIdType.MESH
BF16 = jnp.bfloat16
F32 = jnp.float32


def kernel(
    sizes,
    tok_ref, len_ref, gid_ref, gain_ref, gate_ref, up_ref, down_ref, tproj_ref,
    patch_ref, vgain_ref, fc1_ref, fc2_ref, iproj_ref,
    loss_ref, gcap_ref, gimg_ref,
    w_gu, w_dn, w_tp, w_f1, w_f2, w_ip, patches,
    x_buf, xg_buf, p_buf, r_buf, i_buf, q_buf, s_buf, h_buf,
    lens, im1, im1_own, im2, im2_own, imrow, mean_h,
    pin, pd, pdr, emb, embr, outb,
    wsem, tok_ss, xr, ps, pr, iss, ir, qs, qr, hs,
    len_s, len_r, im1_s, im1_r, im2_s, im2_r, pin_s, pin_r, pd_s, pd_r, e_s, e_r, out_s, out_r,
):
    ns, nd, nm = sizes
    grp = nm // nd
    micro, length, piece = tok_ref.shape
    batch = nd * length
    own_rows = batch // nm
    dl = x_buf.shape[2]
    width = gate_ref.shape[2]
    dim = dl * nd
    sec, dp, mp = lax.axis_index("section"), lax.axis_index("dp"), lax.axis_index("mp")
    last = ns - 1
    my_group = mp // grp
    my_q = lax.rem(mp, grp)
    is_final = jnp.logical_and(sec == last, my_group == dp)

    def send(src, dst, s_sem, r_sem, where):
        pltpu.make_async_remote_copy(
            src_ref=src, dst_ref=dst, send_sem=s_sem, recv_sem=r_sem,
            device_id=where, device_id_type=MESH,
        ).start()

    def drain(ref, sem):
        pltpu.make_async_copy(ref, ref, sem).wait()

    def load(src, dst, index):
        pltpu.make_async_copy(src, dst, wsem.at[index]).start()

    def loaded(dst, index):
        pltpu.make_async_copy(dst, dst, wsem.at[index]).wait()

    per = nm // ns

    def token_target(k):
        target = per * sec + k
        home = jnp.logical_and(sec == 0, jnp.logical_and(my_group == dp, target == mp))
        return target, home

    def token_batch(b, _):
        def token_one(k, _):
            target, home = token_target(k)
            dst = x_buf.at[b, pl.ds(pl.multiple_of(dp * length, length), length),
                           pl.ds(pl.multiple_of(my_q * piece, piece), piece)]

            @pl.when(home)
            def _():
                pltpu.make_async_copy(tok_ref.at[b], dst, xr.at[b]).start()

            @pl.when(jnp.logical_not(home))
            def _():
                send(tok_ref.at[b], dst, tok_ss.at[k], xr.at[b], (0, my_group, target))
            return 0

        return lax.fori_loop(0, per, token_one, 0)

    lax.fori_loop(0, micro, token_batch, 0)

    load(patch_ref, patches, 0)
    load(fc1_ref, w_f1, 1)
    load(fc2_ref, w_f2, 2)
    load(gate_ref.at[0], w_gu.at[:, pl.ds(0, width)], 3)
    load(up_ref.at[0], w_gu.at[:, pl.ds(width, width)], 4)
    load(down_ref.at[0], w_dn, 5)
    load(tproj_ref, w_tp, 6)
    load(iproj_ref, w_ip, 7)

    tile_row = lax.broadcasted_iota(jnp.int32, (8, 128), 0)
    my_lens = jnp.ones((8, 128), F32)
    for i in range(micro):
        my_lens = jnp.where(tile_row == i, len_ref[i].astype(F32), my_lens)
    lens[nd - 1] = my_lens

    def dp_peers(body):
        def step(o, _):
            peer = lax.rem(dp + o, nd)
            body(peer, nd - 1 - o)
            return 0

        lax.fori_loop(1, nd, step, 0)

    def slot_of(source):
        return lax.rem(source - dp + 2 * nd - 1, nd)

    dp_peers(lambda peer, slot: send(lens.at[nd - 1], lens.at[slot], len_s, len_r, (sec, peer, mp)))

    loaded(patches, 0)
    loaded(w_f1, 1)
    rows = patches[0].astype(F32)
    scale = lax.rsqrt(jnp.mean(rows * rows, -1, keepdims=True) + 1e-05)
    vnormed = (rows * scale * vgain_ref[...]).astype(BF16)
    hidden = jnp.dot(vnormed, w_f1[...], preferred_element_type=F32)
    vinner = (0.5 * hidden * (1.0 + lax.erf(hidden * (0.5 ** 0.5)))).astype(BF16)
    vsum = jnp.sum(vinner.astype(F32), 0, keepdims=True)
    high = vsum.astype(BF16)
    low = (vsum - high.astype(F32)).astype(BF16)
    loaded(w_f2, 2)
    two = jnp.concatenate([jnp.broadcast_to(high, (8, high.shape[1])), jnp.broadcast_to(low, (8, low.shape[1]))], 0)
    prod = jnp.dot(two, w_f2[...], preferred_element_type=F32)
    part = prod[0:1] + prod[8:9] + jnp.where(mp == 0, 1.0, 0.0) * jnp.sum(rows, 0, keepdims=True)
    vtiles = part.shape[1] // 128
    for i in range(vtiles):
        im1_own[pl.ds(i, 1), :] = part[:, 128 * i:128 * (i + 1)]
    root = grp * lax.rem(dp + 1, nd)

    @pl.when(mp != root)
    def _():
        slot = lax.rem(mp - root - 1 + 2 * nm, nm)
        send(im1_own, im1.at[slot], im1_s, im1_r, (sec, dp, root))

    def image_root():
        @pl.when(mp == root)
        def _():
            drain(im1, im1_r)
            im2_own[...] = im1_own[...] + jnp.sum(im1[...], 0)

            def to_final(t, _):
                d, q = t // grp, lax.rem(t, grp)
                send(im2_own, im2.at[sec * nd + dp], im2_s, im2_r, (last, d, grp * d + q))
                return 0

            lax.fori_loop(0, nd * grp, to_final, 0)

    @pl.when(sec > 0)
    def _():
        image_root()

    loaded(w_gu.at[:, pl.ds(0, width)], 3)
    loaded(w_gu.at[:, pl.ds(width, width)], 4)
    gain = gain_ref[0:1, pl.ds(pl.multiple_of(dp * dl, dl), dl)]

    def chunk(d):
        return pl.ds(pl.multiple_of(d * length, length), length)

    def weights_of(c, b):
        count = lens[slot_of(c), pl.ds(b, 1), :][:, 0:1]
        at = lax.broadcasted_iota(jnp.int32, (length, 1), 0).astype(F32)
        return jnp.where(at < count, 1.0 / count, 0.0)

    def stage_a(b):
        drain(x_buf.at[b], xr.at[b])
        x = x_buf[b].astype(F32)
        total = jnp.sum(x * x, -1, keepdims=True)
        high = total.astype(BF16)
        low = (total - high.astype(F32)).astype(BF16)
        lane = lax.broadcasted_iota(jnp.int32, (batch, 128), 1)
        p_buf[b, :, pl.ds(2 * width, 128)] = jnp.where(
            lane < 64, high.astype(F32), low.astype(F32)).astype(BF16)
        xg_buf[...] = (x * gain).astype(BF16)
        block = 256 if (2 * width) % 256 == 0 else 128

        def columns(j, _):
            at = pl.ds(pl.multiple_of(j * block, block), block)
            p_buf[b, :, at] = jnp.dot(xg_buf[...], w_gu[:, at], preferred_element_type=F32).astype(BF16)
            return 0

        lax.fori_loop(0, 2 * width // block, columns, 0)
        dp_peers(lambda peer, slot: send(
            p_buf.at[b, chunk(peer)], r_buf.at[b, slot], ps.at[b], pr.at[b], (sec, peer, mp)))

    def stage_b(b):
        drain(r_buf.at[b], pr.at[b])
        total = p_buf[b, chunk(dp), :].astype(F32)
        for i in range(nd - 1):
            total = total + r_buf[b, i].astype(F32)
        squares = total[:, 2 * width:2 * width + 1] + total[:, 2 * width + 64:2 * width + 65]
        scale = lax.rsqrt(squares * (1.0 / dim) + 1e-05)
        gate = total[:, :width] * scale
        upper = total[:, width:2 * width] * scale
        inner = (gate * jax.nn.sigmoid(gate) * upper).astype(BF16)

        @pl.when(sec < last)
        def _():
            i_buf[b, chunk(dp), :] = inner
            here = i_buf.at[b, chunk(dp)]
            dp_peers(lambda peer, slot: send(here, here, iss.at[b], ir.at[b], (sec, peer, mp)))

        @pl.when(sec == last)
        def _():
            @pl.when(b == 0)
            def _():
                drain(lens.at[pl.ds(0, nd - 1)], len_r)
                pin[...] = jnp.zeros(pin.shape, F32)
                mean_h[...] = jnp.zeros(mean_h.shape, F32)

            pin[nd - 1, pl.ds(b, 1), :] = jnp.sum(inner.astype(F32) * weights_of(dp, b), 0, keepdims=True)

            @pl.when(is_final)
            def _():
                cols = pl.ds(pl.multiple_of(my_q * piece, piece), piece)
                for c in range(nd):
                    slab = x_buf[b, pl.ds(c * length, length), cols].astype(F32)
                    mean_h[c, pl.ds(b, 1), :] = jnp.sum(slab * weights_of(c, b), 0, keepdims=True)

    def mp_peers(body):
        def step(o, _):
            peer = lax.rem(mp + o, nm)
            body(peer, nm - 1 - o)
            return 0

        lax.fori_loop(1, nm, step, 0)

    def own(j):
        return pl.ds(pl.multiple_of(j * own_rows, own_rows), own_rows)

    def stage_c(b):
        drain(i_buf.at[b, pl.ds(0, batch - length)], ir.at[b])
        q_buf[b] = jnp.dot(i_buf[b], w_dn[...], preferred_element_type=F32).astype(BF16)
        mp_peers(lambda peer, slot: send(
            q_buf.at[b, own(peer)], s_buf.at[b, slot], qs.at[b], qr.at[b], (sec, dp, peer)))

    def stage_d(b):
        drain(s_buf.at[b], qr.at[b])
        total = x_buf[b, own(mp), :].astype(F32) + q_buf[b, own(mp), :].astype(F32)
        for i in range(nm - 1):
            total = total + s_buf[b, i].astype(F32)
        h_buf[b] = total.astype(BF16)

        def onward(o, _):
            send(h_buf.at[b], x_buf.at[b, own(mp)], hs.at[b], xr.at[b], (sec + 1, dp, lax.rem(mp + o, nm)))
            return 0

        lax.fori_loop(0, nm, onward, 0)

    def tick(i, _):
        @pl.when(jnp.logical_and(sec < last, i >= 3))
        def _():
            stage_d(i - 3)

        @pl.when(jnp.logical_and(sec < last, jnp.logical_and(i >= 2, i < micro + 2)))
        def _():
            @pl.when(i == 2)
            def _():
                loaded(w_dn, 5)

            stage_c(i - 2)

        @pl.when(jnp.logical_and(i >= 1, i < micro + 1))
        def _():
            stage_b(i - 1)

        @pl.when(i < micro)
        def _():
            stage_a(i)

        return 0

    lax.fori_loop(0, micro + 3, tick, 0)

    @pl.when(sec == 0)
    def _():
        image_root()

    loaded(w_tp, 6)
    loaded(w_ip, 7)

    @pl.when(sec == last)
    def _():
        loaded(w_dn, 5)
        dp_peers(lambda peer, slot: send(pin.at[nd - 1], pin.at[slot], pin_s, pin_r, (sec, peer, mp)))

        @pl.when(is_final)
        def _():
            drain(im2, im2_r)
            imrow[...] = jnp.zeros(imrow.shape, F32)
            for d in range(nd):
                image = im2[d]
                for s in range(1, ns):
                    image = image + im2[s * nd + d]
                for i in range(vtiles):
                    imrow[d:d + 1, 128 * i:128 * (i + 1)] = image[i:i + 1, :]

        drain(pin.at[pl.ds(0, nd - 1)], pin_r)
        pooled = jnp.concatenate([pin[slot_of(c)] for c in range(nd)], 0).astype(BF16)
        out = jnp.dot(pooled, w_dn[...], preferred_element_type=F32)
        for q in range(grp):
            pd[q] = out[:, q * piece:(q + 1) * piece]

        def to_final(q, _):
            target = grp * dp + q

            @pl.when(target != mp)
            def _():
                slot = lax.rem(mp - target - 1 + 2 * nm, nm)
                send(pd.at[q], pdr.at[slot], pd_s.at[q], pd_r, (sec, dp, target))
            return 0

        lax.fori_loop(0, grp, to_final, 0)

    def fan_target(t):
        s, y = t // nd, lax.rem(t, nd)
        target = y * grp + my_q
        return s, target, jnp.logical_and(s == last, target == mp)

    nf = nd * grp
    me_f = dp * grp + my_q

    @pl.when(is_final)
    def _():
        drain(pdr, pd_r)
        total = pd[my_q]
        for i in range(nm - 1):
            total = total + pdr[i]
        total = total + mean_h[...].reshape(nd * 8, piece)
        emb[...] = jnp.dot(total.astype(BF16), w_tp[...], preferred_element_type=F32)

        def to_others(o, _):
            f = lax.rem(me_f + o, nf)
            d, q = f // grp, lax.rem(f, grp)
            send(emb, embr.at[nf - 1 - o], e_s, e_r, (last, d, grp * d + q))
            return 0

        lax.fori_loop(1, nf, to_others, 0)
        pooled = (imrow[...] * (1.0 / (ns * patch_ref.shape[1]))).astype(BF16)
        image = jnp.dot(pooled, w_ip[...], preferred_element_type=F32)
        iu = image * lax.rsqrt(jnp.sum(image * image, -1, keepdims=True) + 1e-06)

        nrow = nd * 8
        row = lax.broadcasted_iota(jnp.int32, (nrow, 8), 0)
        col = lax.broadcasted_iota(jnp.int32, (nrow, 8), 1)
        gids = jnp.full((nrow, 8), -1, jnp.int32)
        for k in range(nd * micro):
            gids = jnp.where(row == 8 * (k // micro) + k % micro, gid_ref[k], gids)
        match = jnp.where(gids == col, 1.0, 0.0)
        real_row = lax.rem(row, 8) < micro
        real = jnp.where(jnp.logical_and(real_row, col < nd), 1.0, 0.0)

        drain(embr, e_r)
        total = emb[...]
        for i in range(nf - 1):
            total = total + embr[i]
        cu = total * lax.rsqrt(jnp.sum(total * total, -1, keepdims=True) + 1e-06)
        logits = jnp.zeros((nrow, 8), F32)
        for j in range(nd):
            logits = jnp.where(col == j, 10.0 * jnp.sum(cu * iu[j:j + 1], -1, keepdims=True), logits)
        expo = jnp.exp(logits) * real
        good = expo * match
        by_row = jnp.sum(expo, 1, keepdims=True)
        by_row = jnp.where(by_row > 0, by_row, 1.0)
        by_col = jnp.sum(expo, 0, keepdims=True)
        by_col = jnp.where(by_col > 0, by_col, 1.0)
        good_col = jnp.sum(good, 0, keepdims=True)
        good_col = jnp.where(good_col > 0, good_col, 1.0)
        forward = jnp.sum(jnp.log(by_row)) - jnp.sum(logits * match * real)
        backward = jnp.sum(jnp.log(by_col)) - jnp.sum(jnp.log(good_col))
        loss = 0.5 * (forward / (nd * micro) + backward / nd)
        slope = 5.0 * (expo / by_row - match * real + expo / by_col - good / good_col)
        gcap = jnp.zeros(cu.shape, F32)
        gimg = jnp.zeros((1, cu.shape[1]), F32)
        for j in range(nd):
            gcap = gcap + slope[:, j:j + 1] * iu[j:j + 1]
            gimg = gimg + jnp.where(dp == j, 1.0, 0.0) * jnp.sum(slope[:, j:j + 1] * cu, 0, keepdims=True)
        mine = jnp.zeros((8, cu.shape[1]), F32)
        for d in range(nd):
            mine = mine + jnp.where(dp == d, 1.0, 0.0) * gcap[8 * d:8 * d + 8]
        outb[0:8, :] = mine
        outb[8:16, :] = jnp.broadcast_to(gimg, (8, cu.shape[1]))
        outb[16:24, :] = jnp.full((8, cu.shape[1]), loss, F32)

        def fan(t, _):
            s, target, home = fan_target(t)

            @pl.when(jnp.logical_not(home))
            def _():
                send(outb, outb, out_s.at[t], out_r, (s, dp, target))
            return 0

        lax.fori_loop(0, ns * nd, fan, 0)

    @pl.when(jnp.logical_not(is_final))
    def _():
        drain(outb, out_r)

    loss_ref[...] = outb[16:17, 0:128]
    gcap_ref[...] = outb[0:micro, :]
    gimg_ref[...] = outb[8:9, :]

    def sent_tokens(k, _):
        _, home = token_target(k)

        @pl.when(jnp.logical_not(home))
        def _():
            drain(tok_ref, tok_ss.at[k])
        return 0

    lax.fori_loop(0, per, sent_tokens, 0)
    drain(lens.at[pl.ds(0, nd - 1)], len_s)

    @pl.when(sec < last)
    def _():
        drain(lens.at[pl.ds(0, nd - 1)], len_r)

    @pl.when(mp != root)
    def _():
        drain(im1_own, im1_s)

    @pl.when(mp == root)
    def _():
        drain(im2, im2_s)

    def sent_batch(b, _):
        drain(r_buf.at[b], ps.at[b])

        @pl.when(sec < last)
        def _():
            drain(i_buf.at[b, pl.ds(0, batch - length)], iss.at[b])
            drain(s_buf.at[b], qs.at[b])
            drain(x_buf.at[b], hs.at[b])
        return 0

    lax.fori_loop(0, micro, sent_batch, 0)

    @pl.when(sec == last)
    def _():
        drain(pin.at[pl.ds(0, nd - 1)], pin_s)

        def sent_pd(q, _):
            @pl.when(grp * dp + q != mp)
            def _():
                drain(pd.at[0], pd_s.at[q])
            return 0

        lax.fori_loop(0, grp, sent_pd, 0)

    @pl.when(is_final)
    def _():
        drain(embr, e_s)

        def sent_fan(t, _):
            _, _, home = fan_target(t)

            @pl.when(jnp.logical_not(home))
            def _():
                drain(outb, out_s.at[t])
            return 0

        lax.fori_loop(0, ns * nd, sent_fan, 0)


def per_device(
    sizes,
    caption_tokens, caption_lengths, group_ids, text_gain, text_gate, text_up, text_down,
    text_proj, image_patches, image_gain, image_fc1, image_fc2, image_proj,
):
    ns, nd, nm = sizes
    grp = nm // nd
    micro, length, piece = caption_tokens.shape
    batch = nd * length
    own_rows = batch // nm
    dl, width = text_gate.shape[1], text_gate.shape[2]
    dv, hv = image_fc1.shape
    embed = text_proj.shape[1]
    nf = nd * grp
    any_spec = pl.BlockSpec(memory_space=pl.ANY)
    vmem = pl.BlockSpec(memory_space=pltpu.VMEM)
    smem = pl.BlockSpec(memory_space=pltpu.SMEM)
    dma = pltpu.SemaphoreType.DMA
    loss, gcap, gimg = pl.pallas_call(
        functools.partial(kernel, sizes),
        out_shape=(
            jax.ShapeDtypeStruct((1, 128), F32),
            jax.ShapeDtypeStruct((micro, embed), F32),
            jax.ShapeDtypeStruct((1, embed), F32),
        ),
        in_specs=[any_spec, smem, smem, vmem, any_spec, any_spec, any_spec, any_spec,
                  any_spec, vmem, any_spec, any_spec, any_spec],
        out_specs=(vmem, vmem, vmem),
        scratch_shapes=[
            pltpu.VMEM((dl, 2 * width), BF16),
            pltpu.VMEM((width, dl), BF16),
            pltpu.VMEM((piece, embed), BF16),
            pltpu.VMEM((dv, hv), BF16),
            pltpu.VMEM((hv, dv), BF16),
            pltpu.VMEM((dv, embed), BF16),
            pltpu.VMEM(image_patches.shape, BF16),
            pltpu.VMEM((micro, batch, dl), BF16),
            pltpu.VMEM((batch, dl), BF16),
            pltpu.VMEM((micro, batch, 2 * width + 128), BF16),
            pltpu.VMEM((micro, nd - 1, length, 2 * width + 128), BF16),
            pltpu.VMEM((micro, batch, width), BF16),
            pltpu.VMEM((micro, batch, dl), BF16),
            pltpu.VMEM((micro, nm - 1, own_rows, dl), BF16),
            pltpu.VMEM((micro, own_rows, dl), BF16),
            pltpu.VMEM((nd, 8, 128), F32),
            pltpu.VMEM((nm - 1, dv // 128, 128), F32),
            pltpu.VMEM((dv // 128, 128), F32),
            pltpu.VMEM((ns * nd, dv // 128, 128), F32),
            pltpu.VMEM((dv // 128, 128), F32),
            pltpu.VMEM((8, dv), F32),
            pltpu.VMEM((nd, 8, piece), F32),
            pltpu.VMEM((nd, 8, width), F32),
            pltpu.VMEM((grp, nd * 8, piece), F32),
            pltpu.VMEM((nm - 1, nd * 8, piece), F32),
            pltpu.VMEM((nd * 8, embed), F32),
            pltpu.VMEM((nf - 1, nd * 8, embed), F32),
            pltpu.VMEM((24, embed), F32),
            dma((8,)), dma((nm // ns,)), dma((micro,)), dma((micro,)), dma((micro,)), dma((micro,)),
            dma((micro,)), dma((micro,)), dma((micro,)), dma((micro,)),
            dma, dma, dma, dma, dma, dma, dma, dma, dma((grp,)), dma, dma, dma, dma((ns * nd,)), dma,
        ],
        compiler_params=pltpu.CompilerParams(
            has_side_effects=True, vmem_limit_bytes=48 * 2 ** 20),
        name="towers",
    )(
        caption_tokens, caption_lengths, group_ids, text_gain, text_gate, text_up, text_down,
        text_proj, image_patches, image_gain.reshape(1, dv), image_fc1, image_fc2, image_proj,
    )
    return loss[0, 0], gcap, gimg


def solution(mesh):
    sizes = tuple(mesh.shape[axis] for axis in ("section", "dp", "mp"))
    return jax.shard_map(
        functools.partial(per_device, sizes),
        mesh=mesh,
        in_specs=(
            P("dp", None, "mp"),
            P("dp"),
            P(),
            P("section", None),
            P("section", "dp", "mp"),
            P("section", "dp", "mp"),
            P("section", "mp", "dp"),
            P("mp", None),
            P("dp", "section", None),
            P(),
            P(None, "mp"),
            P("mp", None),
            P(),
        ),
        out_specs=(P(), P("dp", None), P("dp", None)),
        check_vma=False,
    )
```

time: 2160 us -> 295 us (0.14); the launches traced: 2120 us -> 293 us
  waiting for transfers between devices: 1570 us -> 0 us
  blocking collectives: 310 us -> 0 us
  Pallas kernels: 0 us -> 280 us
  matrix products: 96.8 us -> 0 us
  starting transfers between devices: 94.3 us -> 0 us
  other arithmetic: 31.2 us -> 0 us
    psum x8 -> x0, waiting for transfers between devices: 1240 us -> none  [the longest x7 1090 us: advance_full(): lax.psum(branch_terms(incoming).astype(jnp.bfloat16), 'mp')]
    psum x2 -> x0, blocking collectives: 291 us -> none  [the longest x1 275 us: per_device(): caption_embed = lax.psum(caption_term, ('section', 'mp'))]
    all_gather x4 -> x0, waiting for transfers between devices: 282 us -> none  [the longest x1 79.6 us: per_device(): lax.all_gather(text_up, 'dp', axis=1, tiled=True)]
    pallas_call x0 -> x1, Pallas kernels: none -> 280 us  [per_device(): pl.pallas_call(functools.partial(kernel, sizes), out_shape=(jax.ShapeDtyp...]
    dot_general x20 -> x0, matrix products: 96.8 us -> none  [the longest x7 61.3 us: branch_terms(): return jnp.dot(inner, down_full, preferred_element_type=jnp.float32)]
    ppermute x7 -> x0, starting transfers between devices: 94 us -> none  [passed_along(): return lax.ppermute(shard, axis, pairs)]
    ppermute x7 -> x0, waiting for transfers between devices: 42.7 us -> none  [passed_along(): return lax.ppermute(shard, axis, pairs)]
  transfers between devices with their start and end apart: 19 -> 0, of which waited for: 19 -> 0; matrix products, arithmetic and copies ran while one was open for 0% -> 0% of each run, Pallas kernels for 0% -> 0%
where the time goes in v1:
time: 295 us; the launch traced here: 293 us
  Pallas kernels  280 us (95%)
  local copies, waits for them, and re-layouts  11.7 us (4%)
    pallas_call x1, Pallas kernels, per_device(): pl.pallas_call(functools.partial(kernel, sizes), out_shape=(jax.ShapeDtyp...  280 us
    unnamed x24, local copies, waits for them, and re-layouts  11.7 us

profile of v1, /device:TPU:1, one launch (start us, length us, event | category | flops | bytes accessed | tf_op | source)
XLA Modules:
  0.0 293.0 jit_solution(1337444625434010368)
XLA Ops:
  0.6 0.0 copy-start
  0.6 1.5 copy-done
  2.1 0.0 copy-start.1
  2.1 1.4 copy-done.1
  3.5 0.0 copy-start.2
  3.5 1.0 copy-done.2
  4.6 0.0 copy-start.3
  4.6 1.0 copy-done.3
  5.6 0.0 copy-start.4
  5.6 1.0 copy-done.4
  6.6 0.0 copy-start.5
  6.6 0.9 copy-done.5
  7.5 0.0 copy-start.6
  7.5 0.9 copy-done.6
  8.4 0.0 copy-start.7
  8.4 0.7 copy-done.7
  9.2 0.0 copy-start.8
  9.2 0.7 copy-done.8
  9.8 0.0 copy-start.9
  9.8 0.7 copy-done.9
  10.5 0.7 copy-done.10
  11.2 279.5 %towers.1 = (f32[1,128]{1,0:T(1,128)S(1)}, f32[4,768]{1,0:T(4,128)S(1)}, f32[1,768]{1,0:T(1,128)S(1)}) custom-call(bf16[4,64,256]{2,1,0:T(8,128)(2,1)S(1)} %copy-done.5, s32[4]{0:T(128)S(1)} %copy-done.9, s32[16]{0:T(128)S(1)} %copy-done.10, f32[1,4096]{1,0:T(1,128)S(1)} %copy-done.7, bf16[1,1024,896]{2,1,0:T(8,128)(2,1)S(1)} %copy-done, ...), custom_call_target="tpu_custom_call" | custom-call | tf_op jit(solution)/shard_map/towers/pallas_call | solution.py:481
  290.7 0.6 copy.20
  291.3 0.6 copy.21
  (1 shorter events, 0.0 us)
Async XLA Ops:
  0.6 1.5 copy-start
  2.1 1.4 copy-start.1
  3.5 1.0 copy-start.2
  4.6 1.0 copy-start.3
  5.6 1.0 copy-start.4
  6.6 0.9 copy-start.5
  7.5 0.9 copy-start.6
  8.4 0.7 copy-start.7
  9.2 0.7 copy-start.8
  9.8 0.7 copy-start.9
  10.5 0.7 copy-start.10

commit v2 on v1

v2 whole, which is shorter than its diff:
```python
import functools

import jax
import jax.numpy as jnp
from jax import lax
from jax.experimental import pallas as pl
from jax.experimental.pallas import tpu as pltpu
from jax.sharding import PartitionSpec as P

MESH = pl.DeviceIdType.MESH
PLANS = ((2, 256), (2, 320), (2, 384), (2, 512))
BF16 = jnp.bfloat16
F32 = jnp.float32


def kernel(
    sizes,
    tok_ref, len_ref, gid_ref, gain_ref, gate_ref, up_ref, down_ref, tproj_ref,
    patch_ref, vgain_ref, fc1_ref, fc2_ref, iproj_ref,
    loss_ref, gcap_ref, gimg_ref,
    w_gu, w_dn, w_tp, w_f1, w_f2, w_ip, patches,
    tok_buf, x_buf, xg_buf, p_buf, ra_buf, rb_buf, r_buf, i_buf, q_buf, t_buf, u_buf, s_buf, h_buf,
    im1, im1_own, im2, im2_own, imrow, mean_h,
    pin, pin_o, pd, pdr, emb, embr, outb,
    wsem, tok_ss, xz, xy, es, pa_s, pa_r, pb_s, pb_r, pc_s, pc_r, pd_s2, pd_r2,
    iss, ir, qs, qr, us, ur, hs,
    tok_r, cs, im1_s, im1_r, im2_s, im2_r, pin_s, pin_r, pd_s, pd_r, e_s, e_r, out_s, out_r,
):
    ns, nd, nm = sizes
    grp = nm // nd
    caps, slots, piece = tok_ref.shape
    ncap = nd * caps
    micro, batch, dl = x_buf.shape
    length = batch // nd
    strip = piece // 2
    width = gate_ref.shape[2]
    dim = dl * nd
    sec, dp, mp = lax.axis_index("section"), lax.axis_index("dp"), lax.axis_index("mp")
    last = ns - 1
    my_group = mp // grp
    my_q = lax.rem(mp, grp)
    is_final = jnp.logical_and(sec == last, my_group == dp)

    def send(src, dst, s_sem, r_sem, where):
        pltpu.make_async_remote_copy(
            src_ref=src, dst_ref=dst, send_sem=s_sem, recv_sem=r_sem,
            device_id=where, device_id_type=MESH,
        ).start()

    def drain(ref, sem):
        pltpu.make_async_copy(ref, ref, sem).wait()

    def load(src, dst, index):
        pltpu.make_async_copy(src, dst, wsem.at[index]).start()

    def loaded(dst, index):
        pltpu.make_async_copy(dst, dst, wsem.at[index]).wait()

    def chunk(d):
        return pl.ds(pl.multiple_of(d * length, length), length)

    rows_y = pl.ds(pl.multiple_of(my_group * length, length), length)
    cols_z = pl.ds(pl.multiple_of(my_q * piece, piece), piece)

    token_home = jnp.logical_and(sec == 0, jnp.logical_and(my_group == 0, dp == 0))
    token_src = tok_ref.at[:, :, pl.ds(pl.multiple_of(lax.rem(sec, 2) * strip, strip), strip)]

    @pl.when(token_home)
    def _():
        pltpu.make_async_copy(token_src, tok_buf.at[dp], tok_r).start()

    @pl.when(jnp.logical_not(token_home))
    def _():
        send(token_src, tok_buf.at[dp], tok_ss, tok_r, (0, my_group, sec * grp + my_q))

    load(gate_ref.at[0], w_gu.at[:, pl.ds(0, width)], 3)
    load(up_ref.at[0], w_gu.at[:, pl.ds(width, width)], 4)

    load(patch_ref, patches, 0)
    load(fc1_ref, w_f1, 1)
    load(fc2_ref, w_f2, 2)
    load(down_ref.at[0], w_dn, 5)
    load(tproj_ref, w_tp, 6)
    load(iproj_ref, w_ip, 7)

    counts = [len_ref[c] for c in range(ncap)]
    starts = [jnp.int32(0)]
    for c in range(ncap):
        starts.append(starts[-1] + counts[c])

    def dp_peers(body):
        def step(o, _):
            peer = lax.rem(dp + o, nd)
            body(peer, nd - 1 - o)
            return 0

        lax.fori_loop(1, nd, step, 0)

    root = grp * lax.rem(dp + 1, nd)
    vtiles = w_f2.shape[1] // 128

    def image_layer():
        loaded(patches, 0)
        loaded(w_f1, 1)
        rows = patches[0].astype(F32)
        scale = lax.rsqrt(jnp.mean(rows * rows, -1, keepdims=True) + 1e-05)
        vnormed = (rows * scale * vgain_ref[...]).astype(BF16)
        hidden = jnp.dot(vnormed, w_f1[...], preferred_element_type=F32)
        vinner = (0.5 * hidden * (1.0 + lax.erf(hidden * (0.5 ** 0.5)))).astype(BF16)
        vsum = jnp.sum(vinner.astype(F32), 0, keepdims=True)
        high = vsum.astype(BF16)
        low = (vsum - high.astype(F32)).astype(BF16)
        loaded(w_f2, 2)
        two = jnp.concatenate([jnp.broadcast_to(high, (8, high.shape[1])), jnp.broadcast_to(low, (8, low.shape[1]))], 0)
        prod = jnp.dot(two, w_f2[...], preferred_element_type=F32)
        part = prod[0:1] + prod[8:9] + jnp.where(mp == 0, 1.0, 0.0) * jnp.sum(rows, 0, keepdims=True)
        for i in range(vtiles):
            im1_own[pl.ds(i, 1), :] = part[:, 128 * i:128 * (i + 1)]

        @pl.when(mp != root)
        def _():
            slot = lax.rem(mp - root - 1 + 2 * nm, nm)
            send(im1_own, im1.at[slot], im1_s, im1_r, (sec, dp, root))

        @pl.when(mp == root)
        def _():
            drain(im1, im1_r)
            im2_own[...] = im1_own[...] + jnp.sum(im1[...], 0)

            def to_final(t, _):
                d, q = t // grp, lax.rem(t, grp)
                send(im2_own, im2.at[sec * nd + dp], im2_s, im2_r, (last, d, grp * d + q))
                return 0

            lax.fori_loop(0, nd * grp, to_final, 0)

    @pl.when(sec > 0)
    def _():
        image_layer()

    loaded(w_gu.at[:, pl.ds(0, width)], 3)
    loaded(w_gu.at[:, pl.ds(width, width)], 4)
    gain = gain_ref[0:1, pl.ds(pl.multiple_of(dp * dl, dl), dl)]

    def members(first, width):
        row = lax.broadcasted_iota(jnp.int32, (ncap, width), 0)
        token = lax.broadcasted_iota(jnp.int32, (ncap, width), 1) + first
        lo = jnp.zeros((ncap, width), jnp.int32)
        hi = jnp.zeros((ncap, width), jnp.int32)
        for c in range(ncap):
            lo = jnp.where(row == c, starts[c], lo)
            hi = jnp.where(row == c, starts[c + 1], hi)
        return jnp.where(jnp.logical_and(token >= lo, token < hi), 1.0, 0.0).astype(BF16)

    right, left, far = lax.rem(dp + 1, nd), lax.rem(dp + nd - 1, nd), lax.rem(dp + 2, nd)
    full = 2 * width + 128
    low_cols, high_cols = pl.ds(0, width), pl.ds(width, width + 128)

    def y_peers(body):
        for o in range(1, nd):
            y = lax.rem(my_group + o, nd)
            body(y, y * grp + my_q, nd - 1 - o)

    def z_peers(body):
        for o in range(1, grp):
            z = lax.rem(my_q + o, grp)
            body(z, my_group * grp + z, grp - 1 - o)

    half_rows = pl.ds(pl.multiple_of((my_group // 2) * (batch // 2), batch // 2), batch // 2)

    def strip_cols(z):
        return pl.ds(pl.multiple_of(z * piece + lax.rem(my_group, 2) * strip, strip), strip)

    def pack():
        pltpu.make_async_copy(tok_buf, tok_buf, tok_r).wait()
        lane = lax.broadcasted_iota(jnp.int32, (8, ncap * slots), 1)
        cap = lane // slots
        pos = jnp.full((8, ncap * slots), -1, jnp.int32)
        for c in range(ncap):
            at = lane - c * slots
            pos = jnp.where(jnp.logical_and(cap == c, at < counts[c]), starts[c] + at, pos)
        tokens = tok_buf[...].reshape(ncap * slots, strip)

        def one(b, _):
            row = lax.broadcasted_iota(jnp.int32, (batch // 2, ncap * slots), 0)
            row = row + (b * batch + (my_group // 2) * (batch // 2))
            picks = jnp.where(row == pos[0:1], 1.0, 0.0).astype(BF16)
            here = x_buf.at[b, half_rows, strip_cols(my_q)]
            x_buf[b, half_rows, strip_cols(my_q)] = jnp.dot(
                picks, tokens, preferred_element_type=F32).astype(BF16)
            z_peers(lambda z, peer, slot: send(here, here, cs.at[b], xz.at[b], (sec, dp, peer)))
            return 0

        lax.fori_loop(0, micro, one, 0)

    @pl.when(sec == 0)
    def _():
        pack()

    def stage_e(b):
        @pl.when(sec == 0)
        def _():
            drain(x_buf.at[b, pl.ds(0, batch // 2), pl.ds(0, (grp - 1) * strip)], xz.at[b])
            for z in range(grp):
                part = x_buf.at[b, half_rows, strip_cols(z)]
                y_peers(lambda y, peer, slot: send(part, part, es.at[b], xy.at[b], (sec, dp, peer)))

        @pl.when(sec > 0)
        def _():
            here = x_buf.at[b, rows_y]
            drain(here, xz.at[b])
            y_peers(lambda y, peer, slot: send(here, here, es.at[b], xy.at[b], (sec, dp, peer)))

    def stage_a(b):
        drain(x_buf.at[b, pl.ds(0, batch - length)], xy.at[b])
        x = x_buf[b].astype(F32)
        total = jnp.sum(x * x, -1, keepdims=True)
        high = total.astype(BF16)
        low = (total - high.astype(F32)).astype(BF16)
        lane = lax.broadcasted_iota(jnp.int32, (batch, 128), 1)
        p_buf[b, :, pl.ds(2 * width, 128)] = jnp.where(
            lane < 64, high.astype(F32), low.astype(F32)).astype(BF16)
        xg_buf[...] = (x * gain).astype(BF16)
        p_buf[b, :, pl.ds(0, 2 * width)] = jnp.dot(
            xg_buf[...], w_gu[...], preferred_element_type=F32).astype(BF16)
        send(p_buf.at[b, chunk(far), low_cols], ra_buf.at[b], pa_s.at[b], pa_r.at[b], (sec, right, mp))
        send(p_buf.at[b, chunk(far), high_cols], rb_buf.at[b], pb_s.at[b], pb_r.at[b], (sec, left, mp))

    def stage_a2(b):
        drain(ra_buf.at[b], pa_r.at[b])
        p_buf[b, chunk(right), low_cols] = (
            p_buf[b, chunk(right), low_cols].astype(F32) + ra_buf[b].astype(F32)).astype(BF16)
        send(p_buf.at[b, chunk(right)], r_buf.at[b, 0], pc_s.at[b], pc_r.at[b], (sec, right, mp))
        drain(rb_buf.at[b], pb_r.at[b])
        p_buf[b, chunk(left), high_cols] = (
            p_buf[b, chunk(left), high_cols].astype(F32) + rb_buf[b].astype(F32)).astype(BF16)
        send(p_buf.at[b, chunk(left)], r_buf.at[b, 1], pd_s2.at[b], pd_r2.at[b], (sec, left, mp))

    def stage_b(b):
        drain(r_buf.at[b, 0], pc_r.at[b])
        drain(r_buf.at[b, 1], pd_r2.at[b])
        total = p_buf[b, chunk(dp), :].astype(F32) + r_buf[b, 0].astype(F32) + r_buf[b, 1].astype(F32)
        squares = total[:, 2 * width:2 * width + 1] + total[:, 2 * width + 64:2 * width + 65]
        scale = lax.rsqrt(squares * (1.0 / dim) + 1e-05)
        gate = total[:, :width] * scale
        upper = total[:, width:2 * width] * scale
        inner = (gate * jax.nn.sigmoid(gate) * upper).astype(BF16)

        @pl.when(sec < last)
        def _():
            i_buf[b, chunk(dp), :] = inner
            here = i_buf.at[b, chunk(dp)]
            dp_peers(lambda peer, slot: send(here, here, iss.at[b], ir.at[b], (sec, peer, mp)))

        @pl.when(sec == last)
        def _():
            @pl.when(b == 0)
            def _():
                pin[...] = jnp.zeros(pin.shape, F32)
                mean_h[...] = jnp.zeros(mean_h.shape, F32)

            mine = members(b * batch + dp * length, length)
            pin[...] = pin[...] + jnp.dot(mine, inner, preferred_element_type=F32)

            @pl.when(is_final)
            def _():
                mean_h[...] = mean_h[...] + jnp.dot(
                    members(b * batch, batch), x_buf[b, :, cols_z], preferred_element_type=F32)

    def stage_c(b):
        drain(i_buf.at[b, pl.ds(0, batch - length)], ir.at[b])
        q_buf[b] = jnp.dot(i_buf[b], w_dn[...], preferred_element_type=F32).astype(BF16)
        y_peers(lambda y, peer, slot: send(
            q_buf.at[b, chunk(y)], t_buf.at[b, slot], qs.at[b], qr.at[b], (sec, dp, peer)))

    def stage_d1(b):
        drain(t_buf.at[b], qr.at[b])
        total = q_buf[b, rows_y, :].astype(F32)
        for i in range(nd - 1):
            total = total + t_buf[b, i].astype(F32)
        u_buf[b] = total.astype(BF16)
        z_peers(lambda z, peer, slot: send(
            u_buf.at[b, :, pl.ds(pl.multiple_of(z * piece, piece), piece)],
            s_buf.at[b, slot], us.at[b], ur.at[b], (sec, dp, peer)))

    def stage_d2(b):
        drain(s_buf.at[b], ur.at[b])
        total = x_buf[b, rows_y, cols_z].astype(F32) + u_buf[b, :, cols_z].astype(F32)
        for i in range(grp - 1):
            total = total + s_buf[b, i].astype(F32)
        h_buf[b] = total.astype(BF16)
        for z in range(grp):
            send(h_buf.at[b], x_buf.at[b, rows_y, cols_z], hs.at[b], xz.at[b],
                 (sec + 1, dp, my_group * grp + lax.rem(my_q + z, grp)))

    def tick(i, _):
        def at(stage, back, also=True):
            @pl.when(jnp.logical_and(also, jnp.logical_and(i >= back, i < micro + back)))
            def _():
                stage(i - back)

        inside = sec < last
        at(stage_d2, 2, inside)
        at(stage_b, 1)
        at(stage_e, 0)

        @pl.when(jnp.logical_and(inside, i == 1))
        def _():
            loaded(w_dn, 5)

        at(stage_c, 1, inside)
        at(stage_a, 0)
        at(stage_d1, 1, inside)
        at(stage_a2, 0)
        return 0

    lax.fori_loop(0, micro + 2, tick, 0)

    @pl.when(sec == 0)
    def _():
        image_layer()

    loaded(w_tp, 6)
    loaded(w_ip, 7)

    def shares():
        row = lax.broadcasted_iota(jnp.int32, (ncap, 1), 0)
        count = jnp.ones((ncap, 1), F32)
        for c in range(ncap):
            count = jnp.where(row == c, counts[c].astype(F32), count)
        return 1.0 / count

    @pl.when(sec == last)
    def _():
        loaded(w_dn, 5)
        pin_o[nd - 1] = (pin[...] * shares()).astype(BF16)
        dp_peers(lambda peer, slot: send(pin_o.at[nd - 1], pin_o.at[slot], pin_s, pin_r, (sec, peer, mp)))

        @pl.when(is_final)
        def _():
            drain(im2, im2_r)
            imrow[...] = jnp.zeros(imrow.shape, F32)
            for d in range(nd):
                image = im2[d]
                for s in range(1, ns):
                    image = image + im2[s * nd + d]
                for i in range(vtiles):
                    imrow[d:d + 1, 128 * i:128 * (i + 1)] = image[i:i + 1, :]

        drain(pin_o.at[pl.ds(0, nd - 1)], pin_r)
        pooled = pin_o[0].astype(F32)
        for i in range(1, nd):
            pooled = pooled + pin_o[i].astype(F32)
        out = jnp.dot(pooled.astype(BF16), w_dn[...], preferred_element_type=F32)
        for q in range(grp):
            pd[q] = out[:, q * piece:(q + 1) * piece]

        def to_final(q, _):
            target = grp * dp + q

            @pl.when(target != mp)
            def _():
                slot = lax.rem(mp - target - 1 + 2 * nm, nm)
                send(pd.at[q], pdr.at[slot], pd_s.at[q], pd_r, (sec, dp, target))
            return 0

        lax.fori_loop(0, grp, to_final, 0)

    def fan_target(t):
        s, y = t // nd, lax.rem(t, nd)
        target = y * grp + my_q
        return s, target, jnp.logical_and(s == last, target == mp)

    nf = nd * grp
    me_f = dp * grp + my_q

    @pl.when(is_final)
    def _():
        drain(pdr, pd_r)
        total = pd[my_q]
        for i in range(nm - 1):
            total = total + pdr[i]
        total = total + mean_h[...] * shares()
        emb[...] = jnp.dot(total.astype(BF16), w_tp[...], preferred_element_type=F32).astype(BF16)

        def to_others(o, _):
            f = lax.rem(me_f + o, nf)
            d, q = f // grp, lax.rem(f, grp)
            send(emb, embr.at[nf - 1 - o], e_s, e_r, (last, d, grp * d + q))
            return 0

        lax.fori_loop(1, nf, to_others, 0)
        pooled = (imrow[...] * (1.0 / (ns * patch_ref.shape[1]))).astype(BF16)
        image = jnp.dot(pooled, w_ip[...], preferred_element_type=F32)
        iu = image * lax.rsqrt(jnp.sum(image * image, -1, keepdims=True) + 1e-06)

        nrow = ncap
        row = lax.broadcasted_iota(jnp.int32, (nrow, 8), 0)
        col = lax.broadcasted_iota(jnp.int32, (nrow, 8), 1)
        gids = jnp.full((nrow, 8), -1, jnp.int32)
        for k in range(ncap):
            gids = jnp.where(row == k, gid_ref[k], gids)
        match = jnp.where(gids == col, 1.0, 0.0)
        real = jnp.where(col < nd, 1.0, 0.0)

        drain(embr, e_r)
        total = emb[...].astype(F32)
        for i in range(nf - 1):
            total = total + embr[i].astype(F32)
        cu = total * lax.rsqrt(jnp.sum(total * total, -1, keepdims=True) + 1e-06)
        logits = jnp.zeros((nrow, 8), F32)
        for j in range(nd):
            logits = jnp.where(col == j, 10.0 * jnp.sum(cu * iu[j:j + 1], -1, keepdims=True), logits)
        expo = jnp.exp(logits) * real
        good = expo * match
        by_row = jnp.sum(expo, 1, keepdims=True)
        by_row = jnp.where(by_row > 0, by_row, 1.0)
        by_col = jnp.sum(expo, 0, keepdims=True)
        by_col = jnp.where(by_col > 0, by_col, 1.0)
        good_col = jnp.sum(good, 0, keepdims=True)
        good_col = jnp.where(good_col > 0, good_col, 1.0)
        forward = jnp.sum(jnp.log(by_row)) - jnp.sum(logits * match * real)
        backward = jnp.sum(jnp.log(by_col)) - jnp.sum(jnp.log(good_col))
        loss = 0.5 * (forward / ncap + backward / nd)
        slope = 5.0 * (expo / by_row - match * real + expo / by_col - good / good_col)
        gcap = jnp.zeros(cu.shape, F32)
        gimg = jnp.zeros((1, cu.shape[1]), F32)
        for j in range(nd):
            gcap = gcap + slope[:, j:j + 1] * iu[j:j + 1]
            gimg = gimg + jnp.where(dp == j, 1.0, 0.0) * jnp.sum(slope[:, j:j + 1] * cu, 0, keepdims=True)
        mine = jnp.zeros((caps, cu.shape[1]), F32)
        for d in range(nd):
            mine = mine + jnp.where(dp == d, 1.0, 0.0) * gcap[caps * d:caps * d + caps]
        outb[0:caps, :] = mine
        outb[8:16, :] = jnp.broadcast_to(gimg, (8, cu.shape[1]))
        outb[16:24, :] = jnp.full((8, cu.shape[1]), loss, F32)

        def fan(t, _):
            s, target, home = fan_target(t)

            @pl.when(jnp.logical_not(home))
            def _():
                send(outb, outb, out_s.at[t], out_r, (s, dp, target))
            return 0

        lax.fori_loop(0, ns * nd, fan, 0)

    @pl.when(jnp.logical_not(is_final))
    def _():
        drain(outb, out_r)

    loss_ref[...] = outb[16:17, 0:128]
    gcap_ref[...] = outb[0:caps, :]
    gimg_ref[...] = outb[8:9, :]

    @pl.when(jnp.logical_not(token_home))
    def _():
        drain(tok_buf.at[0], tok_ss)

    @pl.when(mp != root)
    def _():
        drain(im1_own, im1_s)

    @pl.when(mp == root)
    def _():
        drain(im2, im2_s)

    def sent_batch(b, _):
        drain(x_buf.at[b, pl.ds(0, batch - length)], es.at[b])

        @pl.when(sec == 0)
        def _():
            drain(x_buf.at[b, pl.ds(0, batch // 2), pl.ds(0, (grp - 1) * strip)], cs.at[b])

        drain(ra_buf.at[b], pa_s.at[b])
        drain(rb_buf.at[b], pb_s.at[b])
        drain(r_buf.at[b, 0], pc_s.at[b])
        drain(r_buf.at[b, 1], pd_s2.at[b])

        @pl.when(sec < last)
        def _():
            drain(i_buf.at[b, pl.ds(0, batch - length)], iss.at[b])
            drain(t_buf.at[b], qs.at[b])
            drain(s_buf.at[b], us.at[b])
            drain(x_buf.at[b, rows_y], hs.at[b])
        return 0

    lax.fori_loop(0, micro, sent_batch, 0)

    @pl.when(sec == last)
    def _():
        drain(pin_o.at[pl.ds(0, nd - 1)], pin_s)

        def sent_pd(q, _):
            @pl.when(grp * dp + q != mp)
            def _():
                drain(pd.at[0], pd_s.at[q])
            return 0

        lax.fori_loop(0, grp, sent_pd, 0)

    @pl.when(is_final)
    def _():
        drain(embr, e_s)

        def sent_fan(t, _):
            _, _, home = fan_target(t)

            @pl.when(jnp.logical_not(home))
            def _():
                drain(outb, out_s.at[t])
            return 0

        lax.fori_loop(0, ns * nd, sent_fan, 0)


def per_device(
    sizes, plans,
    caption_tokens, caption_lengths, group_ids, text_gain, text_gate, text_up, text_down,
    text_proj, image_patches, image_gain, image_fc1, image_fc2, image_proj,
):
    all_lengths = lax.all_gather(caption_lengths, "dp", axis=0, tiled=True)
    counted = jnp.sum(all_lengths)
    room = [micro * batch for micro, batch in plans]
    which = sum((counted > r).astype(jnp.int32) for r in room[:-1])
    operands = (
        caption_tokens, all_lengths, group_ids, text_gain, text_gate, text_up, text_down,
        text_proj, image_patches, image_gain.reshape(1, -1), image_fc1, image_fc2, image_proj,
    )
    return lax.switch(which, [functools.partial(towers, sizes, plan) for plan in plans], *operands)


def towers(
    sizes, plan,
    caption_tokens, caption_lengths, group_ids, text_gain, text_gate, text_up, text_down,
    text_proj, image_patches, image_gain, image_fc1, image_fc2, image_proj,
):
    ns, nd, nm = sizes
    grp = nm // nd
    micro, batch = plan
    caps, slots, piece = caption_tokens.shape
    length = batch // nd
    ncap = nd * caps
    dl, width = text_gate.shape[1], text_gate.shape[2]
    dv, hv = image_fc1.shape
    embed = text_proj.shape[1]
    nf = nd * grp
    any_spec = pl.BlockSpec(memory_space=pl.ANY)
    vmem = pl.BlockSpec(memory_space=pltpu.VMEM)
    smem = pl.BlockSpec(memory_space=pltpu.SMEM)
    dma = pltpu.SemaphoreType.DMA
    loss, gcap, gimg = pl.pallas_call(
        functools.partial(kernel, sizes),
        out_shape=(
            jax.ShapeDtypeStruct((1, 128), F32),
            jax.ShapeDtypeStruct((caps, embed), F32),
            jax.ShapeDtypeStruct((1, embed), F32),
        ),
        in_specs=[any_spec, smem, smem, vmem, any_spec, any_spec, any_spec, any_spec,
                  any_spec, vmem, any_spec, any_spec, any_spec],
        out_specs=(vmem, vmem, vmem),
        scratch_shapes=[
            pltpu.VMEM((dl, 2 * width), BF16),
            pltpu.VMEM((width, dl), BF16),
            pltpu.VMEM((piece, embed), BF16),
            pltpu.VMEM((dv, hv), BF16),
            pltpu.VMEM((hv, dv), BF16),
            pltpu.VMEM((dv, embed), BF16),
            pltpu.VMEM(image_patches.shape, BF16),
            pltpu.VMEM((nd, caps, slots, piece // 2), BF16),
            pltpu.VMEM((micro, batch, dl), BF16),
            pltpu.VMEM((batch, dl), BF16),
            pltpu.VMEM((micro, batch, 2 * width + 128), BF16),
            pltpu.VMEM((micro, length, width), BF16),
            pltpu.VMEM((micro, length, width + 128), BF16),
            pltpu.VMEM((micro, 2, length, 2 * width + 128), BF16),
            pltpu.VMEM((micro, batch, width), BF16),
            pltpu.VMEM((micro, batch, dl), BF16),
            pltpu.VMEM((micro, nd - 1, length, dl), BF16),
            pltpu.VMEM((micro, length, dl), BF16),
            pltpu.VMEM((micro, grp - 1, length, piece), BF16),
            pltpu.VMEM((micro, length, piece), BF16),
            pltpu.VMEM((nm - 1, dv // 128, 128), F32),
            pltpu.VMEM((dv // 128, 128), F32),
            pltpu.VMEM((ns * nd, dv // 128, 128), F32),
            pltpu.VMEM((dv // 128, 128), F32),
            pltpu.VMEM((8, dv), F32),
            pltpu.VMEM((ncap, piece), F32),
            pltpu.VMEM((ncap, width), F32),
            pltpu.VMEM((nd, ncap, width), BF16),
            pltpu.VMEM((grp, ncap, piece), F32),
            pltpu.VMEM((nm - 1, ncap, piece), F32),
            pltpu.VMEM((ncap, embed), BF16),
            pltpu.VMEM((nf - 1, ncap, embed), BF16),
            pltpu.VMEM((24, embed), F32),
            dma((8,)), dma, *([dma((micro,))] * 18),
            dma, dma((micro,)), dma, dma, dma, dma, dma, dma, dma((grp,)), dma, dma, dma, dma((ns * nd,)), dma,
        ],
        compiler_params=pltpu.CompilerParams(
            has_side_effects=True, vmem_limit_bytes=60 * 2 ** 20),
        name=f"towers_{micro}_{batch}",
    )(
        caption_tokens, caption_lengths, group_ids, text_gain, text_gate, text_up, text_down,
        text_proj, image_patches, image_gain, image_fc1, image_fc2, image_proj,
    )
    return loss[0, 0], gcap, gimg


def solution(mesh):
    sizes = tuple(mesh.shape[axis] for axis in ("section", "dp", "mp"))
    return jax.shard_map(
        functools.partial(per_device, sizes, PLANS),
        mesh=mesh,
        in_specs=(
            P("dp", None, "mp"),
            P("dp"),
            P(),
            P("section", None),
            P("section", "dp", "mp"),
            P("section", "dp", "mp"),
            P("section", "mp", "dp"),
            P("mp", None),
            P("dp", "section", None),
            P(),
            P(None, "mp"),
            P("mp", None),
            P(),
        ),
        out_specs=(P(), P("dp", None), P("dp", None)),
        check_vma=False,
    )
```

time: 295 us -> 239 us (0.81)
  Pallas kernels: 280 us -> 221 us
  local copies, waits for them, and re-layouts: 11.7 us -> 3.31 us
  blocking collectives: 0 us -> 7.69 us
  between operations: 1.83 us -> 4.99 us
    pallas_call x1, Pallas kernels: 280 us -> 221 us  [towers(): pl.pallas_call(functools.partial(kernel, sizes), out_shape=(jax.ShapeDtyp...]
    unnamed x24 -> x5, local copies, waits for them, and re-layouts: 11.7 us -> 3.31 us
    unnamed x0 -> x1, blocking collectives: none -> 7.69 us
where the time goes in v2:
time: 239 us; the launch traced here: 238 us
  Pallas kernels  221 us (92%)
  blocking collectives  7.69 us (3%)
  between operations  4.99 us (2%)
  local copies, waits for them, and re-layouts  3.31 us (1%)
    pallas_call x1, Pallas kernels, towers(): pl.pallas_call(functools.partial(kernel, sizes), out_shape=(jax.ShapeDtyp...  221 us
    unnamed x1, blocking collectives  7.69 us

profile of v2, /device:TPU:1, one launch (start us, length us, event | category | flops | bytes accessed | tf_op | source)
XLA Modules:
  0.0 238.1 jit_solution(7910734372797885247)
XLA Ops:
  0.6 1.3 dynamic-slice
  2.6 0.9 dynamic-update-slice
  3.4 7.7 %all-reduce = s32[16]{0:T(128)S(1)} all-reduce(s32[16]{0:T(128)S(1)} %dynamic-update-slice), channel_id=1, replica_groups=mesh['section'=4,'dp'=4,'mp'=16] {'dp'}, use_global_device_ids=true, to_apply=%add | all-reduce | flops 16 | bytes 128
  11.1 0.6 reduce_sum.9
  13.7 221.4 %conditional.1 = (f32[4,768]{1,0:T(4,128)S(1)}, f32[1,768]{1,0:T(1,128)S(1)}, f32[]{:T(128)}) conditional(s32[]{:T(128)} %clamp.3, (bf16[4,64,256]{2,1,0:T(8,128)(2,1)}, s32[16]{0:T(128)S(1)}, s32[16]{0:T(128)}, f32[1,4096]{1,0:T(1,128)}, bf16[1,1024,896]{2,1,0:T(8,128)(2,1)}, ...), branch_computations={%region_1.0_spmd, %region_2.0_spmd, %region_3.0_spmd, %region_4.0_... | conditional | bytes 24 | solution.py:530
  13.7 221.2 %towers_2_320.1 = (f32[1,128]{1,0:T(1,128)}, f32[4,768]{1,0:T(4,128)S(1)}, f32[1,768]{1,0:T(1,128)S(1)}) custom-call(bf16[4,64,256]{2,1,0:T(8,128)(2,1)} %get-tuple-element.120.tok_ref, s32[16]{0:T(128)S(1)} %get-tuple-element.121.len_ref, s32[16]{0:T(128)} %get-tuple-element.122.gid_ref, f32[1,4096]{1,0:T(1,128)} %get-tuple-element.123.gain_ref, ...), custom_call_target="tpu_custom_call" | custom-call | tf_op jit(solution)/shard_map/cond/branch_1_fun/towers_2_320/pallas_call | solution.py:552
  235.8 0.6 copy.37
  236.4 0.6 copy.38
  (1 shorter events, 0.0 us)

commit v3 on v2

--- a/solution.py
+++ b/solution.py
@@ -8,7 +8,7 @@
 from jax.sharding import PartitionSpec as P
 
 MESH = pl.DeviceIdType.MESH
-PLANS = ((2, 256), (2, 320), (2, 384), (2, 512))
+PLANS = ((3, 128), (4, 128), (3, 192), (5, 128), (4, 192), (4, 256))
 BF16 = jnp.bfloat16
 F32 = jnp.float32
 
@@ -19,20 +19,20 @@
     patch_ref, vgain_ref, fc1_ref, fc2_ref, iproj_ref,
     loss_ref, gcap_ref, gimg_ref,
     w_gu, w_dn, w_tp, w_f1, w_f2, w_ip, patches,
-    tok_buf, x_buf, xg_buf, p_buf, ra_buf, rb_buf, r_buf, i_buf, q_buf, t_buf, u_buf, s_buf, h_buf,
+    tok_buf, x_buf, far_buf, p_buf, ra_buf, rb_buf, r_buf, i_buf, q_buf, s_buf, h_buf,
     im1, im1_own, im2, im2_own, imrow, mean_h,
     pin, pin_o, pd, pdr, emb, embr, outb,
-    wsem, tok_ss, xz, xy, es, pa_s, pa_r, pb_s, pb_r, pc_s, pc_r, pd_s2, pd_r2,
-    iss, ir, qs, qr, us, ur, hs,
-    tok_r, cs, im1_s, im1_r, im2_s, im2_r, pin_s, pin_r, pd_s, pd_r, e_s, e_r, out_s, out_r,
+    wsem, xr, pa_s, pa_r, pb_s, pb_r, pc_s, pc_r, pd_s2, pd_r2,
+    iss, qs, qr, hs, ir,
+    cs, im1_s, im1_r, im2_s, im2_r, pin_s, pin_r, pd_s, pd_r, e_s, e_r, out_s, out_r,
 ):
     ns, nd, nm = sizes
     grp = nm // nd
-    caps, slots, piece = tok_ref.shape
+    _, caps, slots, strip = tok_ref.shape
+    piece = 2 * strip
     ncap = nd * caps
     micro, batch, dl = x_buf.shape
     length = batch // nd
-    strip = piece // 2
     width = gate_ref.shape[2]
     dim = dl * nd
     sec, dp, mp = lax.axis_index("section"), lax.axis_index("dp"), lax.axis_index("mp")
@@ -62,29 +62,62 @@
     rows_y = pl.ds(pl.multiple_of(my_group * length, length), length)
     cols_z = pl.ds(pl.multiple_of(my_q * piece, piece), piece)
 
-    token_home = jnp.logical_and(sec == 0, jnp.logical_and(my_group == 0, dp == 0))
-    token_src = tok_ref.at[:, :, pl.ds(pl.multiple_of(lax.rem(sec, 2) * strip, strip), strip)]
-
-    @pl.when(token_home)
-    def _():
-        pltpu.make_async_copy(token_src, tok_buf.at[dp], tok_r).start()
-
-    @pl.when(jnp.logical_not(token_home))
-    def _():
-        send(token_src, tok_buf.at[dp], tok_ss, tok_r, (0, my_group, sec * grp + my_q))
+    root = grp * lax.rem(dp + 1, nd)
+    nf = nd * grp
+    me_f = dp * grp + my_q
+    final_mp = dp * grp + my_q
+    barrier = pltpu.get_barrier_semaphore()
+
+    def hello(where):
+        pl.semaphore_signal(barrier, inc=1, device_id=where, device_id_type=MESH)
+
+    def each(lo, hi, body):
+        def step(o, _):
+            body(o)
+            return 0
+
+        lax.fori_loop(lo, hi, step, 0)
+
+    each(1, nd, lambda o: hello((sec, lax.rem(dp + o, nd), mp)))
+    each(1, nm, lambda o: hello((sec, dp, lax.rem(mp + o, nm))))
+
+    @pl.when(sec > 0)
+    def _():
+        each(0, nm, lambda o: hello((sec - 1, dp, lax.rem(mp + o, nm))))
+
+    @pl.when(is_final)
+    def _():
+        each(0, ns * nd, lambda o: hello((o // nd, lax.rem(o, nd), grp * lax.rem(o + 1, nd))))
+
+        def other_final(o):
+            f = lax.rem(me_f + o, nf)
+            hello((last, f // grp, f))
+
+        each(1, nf, other_final)
+
+    @pl.when(jnp.logical_not(is_final))
+    def _():
+        hello((last, dp, final_mp))
+
+    @pl.when(sec == 0)
+    def _():
+        load(tok_ref, tok_buf, 0)
 
     load(gate_ref.at[0], w_gu.at[:, pl.ds(0, width)], 3)
     load(up_ref.at[0], w_gu.at[:, pl.ds(width, width)], 4)
 
-    load(patch_ref, patches, 0)
+    load(patch_ref, patches, 8)
     load(fc1_ref, w_f1, 1)
     load(fc2_ref, w_f2, 2)
     load(down_ref.at[0], w_dn, 5)
     load(tproj_ref, w_tp, 6)
     load(iproj_ref, w_ip, 7)
-
-    counts = [len_ref[c] for c in range(ncap)]
-    starts = [jnp.int32(0)]
+    partners = nd - 1 + nm - 1 + jnp.where(sec < last, nm, 0) + jnp.where(mp == root, nd * grp, 0)
+    partners = partners + jnp.where(is_final, nf - 1 + ns * nd - 1, 0)
+    pl.semaphore_wait(barrier, partners)
+
+    counts = [len_ref[c // caps, c % caps:c % caps + 1, 0:1] for c in range(ncap)]
+    starts = [jnp.zeros((1, 1), F32)]
     for c in range(ncap):
         starts.append(starts[-1] + counts[c])
 
@@ -96,11 +129,10 @@
 
         lax.fori_loop(1, nd, step, 0)
 
-    root = grp * lax.rem(dp + 1, nd)
     vtiles = w_f2.shape[1] // 128
 
     def image_layer():
-        loaded(patches, 0)
+        loaded(patches, 8)
         loaded(w_f1, 1)
         rows = patches[0].astype(F32)
         scale = lax.rsqrt(jnp.mean(rows * rows, -1, keepdims=True) + 1e-05)
@@ -144,9 +176,9 @@
 
     def members(first, width):
         row = lax.broadcasted_iota(jnp.int32, (ncap, width), 0)
-        token = lax.broadcasted_iota(jnp.int32, (ncap, width), 1) + first
-        lo = jnp.zeros((ncap, width), jnp.int32)
-        hi = jnp.zeros((ncap, width), jnp.int32)
+        token = (lax.broadcasted_iota(jnp.int32, (ncap, width), 1) + first).astype(F32)
+        lo = jnp.zeros((ncap, width), F32)
+        hi = jnp.zeros((ncap, width), F32)
         for c in range(ncap):
             lo = jnp.where(row == c, starts[c], lo)
             hi = jnp.where(row == c, starts[c + 1], hi)
@@ -156,39 +188,36 @@
     full = 2 * width + 128
     low_cols, high_cols = pl.ds(0, width), pl.ds(width, width + 128)
 
-    def y_peers(body):
-        for o in range(1, nd):
-            y = lax.rem(my_group + o, nd)
-            body(y, y * grp + my_q, nd - 1 - o)
-
-    def z_peers(body):
-        for o in range(1, grp):
-            z = lax.rem(my_q + o, grp)
-            body(z, my_group * grp + z, grp - 1 - o)
+    def mp_peers(body):
+        def step(o, _):
+            peer = lax.rem(mp + o, nm)
+            body(peer, nm - 1 - o)
+            return 0
+
+        lax.fori_loop(1, nm, step, 0)
 
     half_rows = pl.ds(pl.multiple_of((my_group // 2) * (batch // 2), batch // 2), batch // 2)
 
-    def strip_cols(z):
-        return pl.ds(pl.multiple_of(z * piece + lax.rem(my_group, 2) * strip, strip), strip)
+    strip_cols = pl.ds(pl.multiple_of(my_q * piece + lax.rem(my_group, 2) * strip, strip), strip)
 
     def pack():
-        pltpu.make_async_copy(tok_buf, tok_buf, tok_r).wait()
+        loaded(tok_buf, 0)
         lane = lax.broadcasted_iota(jnp.int32, (8, ncap * slots), 1)
         cap = lane // slots
-        pos = jnp.full((8, ncap * slots), -1, jnp.int32)
+        pos = jnp.full((8, ncap * slots), -1.0, F32)
         for c in range(ncap):
-            at = lane - c * slots
+            at = (lane - c * slots).astype(F32)
             pos = jnp.where(jnp.logical_and(cap == c, at < counts[c]), starts[c] + at, pos)
         tokens = tok_buf[...].reshape(ncap * slots, strip)
 
         def one(b, _):
             row = lax.broadcasted_iota(jnp.int32, (batch // 2, ncap * slots), 0)
-            row = row + (b * batch + (my_group // 2) * (batch // 2))
+            row = (row + (b * batch + (my_group // 2) * (batch // 2))).astype(F32)
             picks = jnp.where(row == pos[0:1], 1.0, 0.0).astype(BF16)
-            here = x_buf.at[b, half_rows, strip_cols(my_q)]
-            x_buf[b, half_rows, strip_cols(my_q)] = jnp.dot(
+            here = x_buf.at[b, half_rows, strip_cols]
+            x_buf[b, half_rows, strip_cols] = jnp.dot(
                 picks, tokens, preferred_element_type=F32).astype(BF16)
-            z_peers(lambda z, peer, slot: send(here, here, cs.at[b], xz.at[b], (sec, dp, peer)))
+            mp_peers(lambda peer, slot: send(here, here, cs.at[b], xr.at[b], (sec, dp, peer)))
             return 0
 
         lax.fori_loop(0, micro, one, 0)
@@ -197,49 +226,46 @@
     def _():
         pack()
 
-    def stage_e(b):
+    def products(rows, out):
+        x = rows.astype(F32)
+        total = jnp.sum(x * x, -1, keepdims=True)
+        high = total.astype(BF16).astype(F32)
+        lane = lax.broadcasted_iota(jnp.int32, (x.shape[0], 128), 1)
+        out[:, pl.ds(2 * width, 128)] = jnp.where(lane < 64, high, total - high).astype(BF16)
+        out[:, pl.ds(0, 2 * width)] = jnp.dot(
+            (x * gain).astype(BF16), w_gu[...], preferred_element_type=F32).astype(BF16)
+
+    def stage_a(b):
         @pl.when(sec == 0)
         def _():
-            drain(x_buf.at[b, pl.ds(0, batch // 2), pl.ds(0, (grp - 1) * strip)], xz.at[b])
-            for z in range(grp):
-                part = x_buf.at[b, half_rows, strip_cols(z)]
-                y_peers(lambda y, peer, slot: send(part, part, es.at[b], xy.at[b], (sec, dp, peer)))
+            drain(s_buf.at[b], xr.at[b])
 
         @pl.when(sec > 0)
         def _():
-            here = x_buf.at[b, rows_y]
-            drain(here, xz.at[b])
-            y_peers(lambda y, peer, slot: send(here, here, es.at[b], xy.at[b], (sec, dp, peer)))
-
-    def stage_a(b):
-        drain(x_buf.at[b, pl.ds(0, batch - length)], xy.at[b])
-        x = x_buf[b].astype(F32)
-        total = jnp.sum(x * x, -1, keepdims=True)
-        high = total.astype(BF16)
-        low = (total - high.astype(F32)).astype(BF16)
-        lane = lax.broadcasted_iota(jnp.int32, (batch, 128), 1)
-        p_buf[b, :, pl.ds(2 * width, 128)] = jnp.where(
-            lane < 64, high.astype(F32), low.astype(F32)).astype(BF16)
-        xg_buf[...] = (x * gain).astype(BF16)
-        p_buf[b, :, pl.ds(0, 2 * width)] = jnp.dot(
-            xg_buf[...], w_gu[...], preferred_element_type=F32).astype(BF16)
-        send(p_buf.at[b, chunk(far), low_cols], ra_buf.at[b], pa_s.at[b], pa_r.at[b], (sec, right, mp))
-        send(p_buf.at[b, chunk(far), high_cols], rb_buf.at[b], pb_s.at[b], pb_r.at[b], (sec, left, mp))
+            drain(x_buf.at[b], xr.at[b])
+
+        products(x_buf[b, chunk(far), :], far_buf.at[b])
+        send(far_buf.at[b, :, low_cols], ra_buf.at[b], pa_s.at[b], pa_r.at[b], (sec, right, mp))
+        send(far_buf.at[b, :, high_cols], rb_buf.at[b], pb_s.at[b], pb_r.at[b], (sec, left, mp))
+        near = jnp.concatenate([x_buf[b, chunk(c), :] for c in (right, left, dp)], 0)
+        products(near, p_buf.at[b])
+
+    to_right, to_left, to_self = pl.ds(0, length), pl.ds(length, length), pl.ds(2 * length, length)
 
     def stage_a2(b):
         drain(ra_buf.at[b], pa_r.at[b])
-        p_buf[b, chunk(right), low_cols] = (
-            p_buf[b, chunk(right), low_cols].astype(F32) + ra_buf[b].astype(F32)).astype(BF16)
-        send(p_buf.at[b, chunk(right)], r_buf.at[b, 0], pc_s.at[b], pc_r.at[b], (sec, right, mp))
+        p_buf[b, to_right, low_cols] = (
+            p_buf[b, to_right, low_cols].astype(F32) + ra_buf[b].astype(F32)).astype(BF16)
+        send(p_buf.at[b, to_right], r_buf.at[b, 0], pc_s.at[b], pc_r.at[b], (sec, right, mp))
         drain(rb_buf.at[b], pb_r.at[b])
-        p_buf[b, chunk(left), high_cols] = (
-            p_buf[b, chunk(left), high_cols].astype(F32) + rb_buf[b].astype(F32)).astype(BF16)
-        send(p_buf.at[b, chunk(left)], r_buf.at[b, 1], pd_s2.at[b], pd_r2.at[b], (sec, left, mp))
+        p_buf[b, to_left, high_cols] = (
+            p_buf[b, to_left, high_cols].astype(F32) + rb_buf[b].astype(F32)).astype(BF16)
+        send(p_buf.at[b, to_left], r_buf.at[b, 1], pd_s2.at[b], pd_r2.at[b], (sec, left, mp))
 
     def stage_b(b):
         drain(r_buf.at[b, 0], pc_r.at[b])
         drain(r_buf.at[b, 1], pd_r2.at[b])
-        total = p_buf[b, chunk(dp), :].astype(F32) + r_buf[b, 0].astype(F32) + r_buf[b, 1].astype(F32)
+        total = p_buf[b, to_self, :].astype(F32) + r_buf[b, 0].astype(F32) + r_buf[b, 1].astype(F32)
         squares = total[:, 2 * width:2 * width + 1] + total[:, 2 * width + 64:2 * width + 65]
         scale = lax.rsqrt(squares * (1.0 / dim) + 1e-05)
         gate = total[:, :width] * scale
@@ -250,7 +276,8 @@
         def _():
             i_buf[b, chunk(dp), :] = inner
             here = i_buf.at[b, chunk(dp)]
-            dp_peers(lambda peer, slot: send(here, here, iss.at[b], ir.at[b], (sec, peer, mp)))
+            for o in (1, nd - 1, 2):
+                send(here, here, iss.at[b], ir.at[nd - 1 - o, b], (sec, lax.rem(dp + o, nd), mp))
 
         @pl.when(sec == last)
         def _():
@@ -268,30 +295,43 @@
                     members(b * batch, batch), x_buf[b, :, cols_z], preferred_element_type=F32)
 
     def stage_c(b):
-        drain(i_buf.at[b, pl.ds(0, batch - length)], ir.at[b])
-        q_buf[b] = jnp.dot(i_buf[b], w_dn[...], preferred_element_type=F32).astype(BF16)
-        y_peers(lambda y, peer, slot: send(
-            q_buf.at[b, chunk(y)], t_buf.at[b, slot], qs.at[b], qr.at[b], (sec, dp, peer)))
-
-    def stage_d1(b):
-        drain(t_buf.at[b], qr.at[b])
-        total = q_buf[b, rows_y, :].astype(F32)
-        for i in range(nd - 1):
-            total = total + t_buf[b, i].astype(F32)
-        u_buf[b] = total.astype(BF16)
-        z_peers(lambda z, peer, slot: send(
-            u_buf.at[b, :, pl.ds(pl.multiple_of(z * piece, piece), piece)],
-            s_buf.at[b, slot], us.at[b], ur.at[b], (sec, dp, peer)))
-
-    def stage_d2(b):
-        drain(s_buf.at[b], ur.at[b])
-        total = x_buf[b, rows_y, cols_z].astype(F32) + u_buf[b, :, cols_z].astype(F32)
-        for i in range(grp - 1):
+        def from_sources(offsets):
+            sources = [lax.rem(dp + o, nd) for o in offsets]
+            for o, source in zip(offsets, sources):
+                if o:
+                    drain(i_buf.at[b, chunk(source)], ir.at[o - 1, b])
+            out = jnp.dot(jnp.concatenate([i_buf[b, chunk(c), :] for c in sources], 0), w_dn[...],
+                          preferred_element_type=F32).astype(BF16)
+            for at, source in enumerate(sources):
+                q_buf[b, chunk(source), :] = out[at * length:(at + 1) * length]
+
+                def to_owner(z, source=source):
+                    owner = source * grp + z
+
+                    @pl.when(owner != mp)
+                    def _():
+                        slot = lax.rem(mp - owner - 1 + 2 * nm, nm)
+                        send(q_buf.at[b, chunk(source), pl.ds(pl.multiple_of(z * piece, piece), piece)],
+                             s_buf.at[b, slot], qs.at[b], qr.at[b], (sec, dp, owner))
+
+                each(0, grp, to_owner)
+
+        from_sources((0, 1, nd - 1))
+        from_sources((2,))
+
+    def stage_d(b):
+        drain(s_buf.at[b], qr.at[b])
+        total = x_buf[b, rows_y, cols_z].astype(F32) + q_buf[b, rows_y, cols_z].astype(F32)
+        for i in range(nm - 1):
             total = total + s_buf[b, i].astype(F32)
         h_buf[b] = total.astype(BF16)
-        for z in range(grp):
-            send(h_buf.at[b], x_buf.at[b, rows_y, cols_z], hs.at[b], xz.at[b],
-                 (sec + 1, dp, my_group * grp + lax.rem(my_q + z, grp)))
+
+        def onward(o, _):
+            send(h_buf.at[b], x_buf.at[b, rows_y, cols_z], hs.at[b], xr.at[b],
+                 (sec + 1, dp, lax.rem(mp + o, nm)))
+            return 0
+
+        lax.fori_loop(0, nm, onward, 0)
 
     def tick(i, _):
         def at(stage, back, also=True):
@@ -300,17 +340,15 @@
                 stage(i - back)
 
         inside = sec < last
-        at(stage_d2, 2, inside)
+        at(stage_d, 2, inside)
         at(stage_b, 1)
-        at(stage_e, 0)
+        at(stage_a, 0)
 
         @pl.when(jnp.logical_and(inside, i == 1))
         def _():
             loaded(w_dn, 5)
 
         at(stage_c, 1, inside)
-        at(stage_a, 0)
-        at(stage_d1, 1, inside)
         at(stage_a2, 0)
         return 0
 
@@ -327,7 +365,7 @@
         row = lax.broadcasted_iota(jnp.int32, (ncap, 1), 0)
         count = jnp.ones((ncap, 1), F32)
         for c in range(ncap):
-            count = jnp.where(row == c, counts[c].astype(F32), count)
+            count = jnp.where(row == c, counts[c], count)
         return 1.0 / count
 
     @pl.when(sec == last)
@@ -370,9 +408,6 @@
         s, y = t // nd, lax.rem(t, nd)
         target = y * grp + my_q
         return s, target, jnp.logical_and(s == last, target == mp)
-
-    nf = nd * grp
-    me_f = dp * grp + my_q
 
     @pl.when(is_final)
     def _():
@@ -432,8 +467,8 @@
         for d in range(nd):
             mine = mine + jnp.where(dp == d, 1.0, 0.0) * gcap[caps * d:caps * d + caps]
         outb[0:caps, :] = mine
-        outb[8:16, :] = jnp.broadcast_to(gimg, (8, cu.shape[1]))
-        outb[16:24, :] = jnp.full((8, cu.shape[1]), loss, F32)
+        outb[caps:caps + 1, :] = gimg
+        outb[caps + 1:8, :] = jnp.full((7 - caps, cu.shape[1]), loss, F32)
 
         def fan(t, _):
             s, target, home = fan_target(t)
@@ -449,13 +484,9 @@
     def _():
         drain(outb, out_r)
 
-    loss_ref[...] = outb[16:17, 0:128]
+    loss_ref[...] = outb[caps + 1:caps + 2, 0:128]
     gcap_ref[...] = outb[0:caps, :]
-    gimg_ref[...] = outb[8:9, :]
-
-    @pl.when(jnp.logical_not(token_home))
-    def _():
-        drain(tok_buf.at[0], tok_ss)
+    gimg_ref[...] = outb[caps:caps + 1, :]
 
     @pl.when(mp != root)
     def _():
@@ -466,11 +497,9 @@
         drain(im2, im2_s)
 
     def sent_batch(b, _):
-        drain(x_buf.at[b, pl.ds(0, batch - length)], es.at[b])
-
         @pl.when(sec == 0)
         def _():
-            drain(x_buf.at[b, pl.ds(0, batch // 2), pl.ds(0, (grp - 1) * strip)], cs.at[b])
+            drain(s_buf.at[b], cs.at[b])
 
         drain(ra_buf.at[b], pa_s.at[b])
         drain(rb_buf.at[b], pb_s.at[b])
@@ -480,9 +509,8 @@
         @pl.when(sec < last)
         def _():
             drain(i_buf.at[b, pl.ds(0, batch - length)], iss.at[b])
-            drain(t_buf.at[b], qs.at[b])
-            drain(s_buf.at[b], us.at[b])
-            drain(x_buf.at[b, rows_y], hs.at[b])
+            drain(s_buf.at[b], qs.at[b])
+            drain(x_buf.at[b], hs.at[b])
         return 0
 
     lax.fori_loop(0, micro, sent_batch, 0)
@@ -512,6 +540,115 @@
             return 0
 
         lax.fori_loop(0, ns * nd, sent_fan, 0)
+
+
+def front_kernel(sizes, rooms, tok_ref, len_ref, strips_ref, lens_ref, which_ref, lens, len_s, len_r, tok_s, tok_r, home_s):
+    ns, nd, nm = sizes
+    grp = nm // nd
+    caps, _, piece = tok_ref.shape
+    strip = piece // 2
+    sec, dp, mp = lax.axis_index("section"), lax.axis_index("dp"), lax.axis_index("mp")
+    my_group, my_q = mp // grp, lax.rem(mp, grp)
+    home = jnp.logical_and(sec == 0, jnp.logical_and(my_group == 0, dp == 0))
+    want_sec = my_group
+    barrier = pltpu.get_barrier_semaphore()
+
+    def hello(where):
+        pl.semaphore_signal(barrier, inc=1, device_id=where, device_id_type=MESH)
+
+    for o in range(1, nd):
+        hello((sec, lax.rem(dp + o, nd), mp))
+
+    @pl.when(sec == 0)
+    def _():
+        for d in range(nd):
+            @pl.when(jnp.logical_not(jnp.logical_and(want_sec == 0, jnp.logical_and(dp == 0, d == 0))))
+            def _():
+                hello((want_sec, d, dp * grp + my_q))
+
+    row = lax.broadcasted_iota(jnp.int32, (8, 128), 0)
+    mine = jnp.zeros((8, 128), F32)
+    for i in range(caps):
+        mine = jnp.where(row == i, len_ref[i].astype(F32), mine)
+    lens[dp] = mine
+
+    source = tok_ref.at[:, :, pl.ds(pl.multiple_of(lax.rem(sec, 2) * strip, strip), strip)]
+    slab = strips_ref.at[dp]
+
+    @pl.when(home)
+    def _():
+        pltpu.make_async_copy(source, slab, home_s).start()
+        pl.semaphore_wait(barrier, nd - 1)
+
+    @pl.when(jnp.logical_not(home))
+    def _():
+        pl.semaphore_wait(barrier, nd)
+
+    for o in range(1, nd):
+        pltpu.make_async_remote_copy(
+            src_ref=lens.at[dp], dst_ref=lens.at[dp], send_sem=len_s.at[o - 1], recv_sem=len_r.at[nd - 1 - o],
+            device_id=(sec, lax.rem(dp + o, nd), mp), device_id_type=MESH).start()
+
+    @pl.when(jnp.logical_not(home))
+    def _():
+        pltpu.make_async_remote_copy(
+            src_ref=source, dst_ref=slab, send_sem=tok_s, recv_sem=tok_r.at[dp],
+            device_id=(0, my_group, sec * grp + my_q), device_id_type=MESH).start()
+
+    for o in range(1, nd):
+        other = lens.at[lax.rem(dp + o, nd)]
+        pltpu.make_async_copy(other, other, len_r.at[o - 1]).wait()
+    lens_ref[...] = lens[...]
+    counted = jnp.sum(lens[:, :, 0:1])
+    which = jnp.int32(0)
+    for room in rooms[:-1]:
+        which = which + (counted > room).astype(jnp.int32)
+    which_ref[0, 0] = which
+
+    @pl.when(sec == 0)
+    def _():
+        for d in range(nd):
+            here = strips_ref.at[d]
+            itself = jnp.logical_and(want_sec == 0, jnp.logical_and(dp == 0, d == 0))
+
+            @pl.when(itself)
+            def _():
+                pltpu.make_async_copy(here, here, home_s).wait()
+
+            @pl.when(jnp.logical_not(itself))
+            def _():
+                pltpu.make_async_copy(here, here, tok_r.at[d]).wait()
+
+    for o in range(1, nd):
+        pltpu.make_async_copy(lens.at[dp], lens.at[dp], len_s.at[o - 1]).wait()
+
+    @pl.when(jnp.logical_not(home))
+    def _():
+        pltpu.make_async_copy(slab, slab, tok_s).wait()
+
+
+def front(sizes, plans, tokens, lengths):
+    nd = sizes[1]
+    caps, slots, piece = tokens.shape
+    dma = pltpu.SemaphoreType.DMA
+    return pl.pallas_call(
+        functools.partial(front_kernel, sizes, [micro * batch for micro, batch in plans]),
+        out_shape=(
+            jax.ShapeDtypeStruct((nd, caps, slots, piece // 2), BF16),
+            jax.ShapeDtypeStruct((nd, 8, 128), F32),
+            jax.ShapeDtypeStruct((1, 1), jnp.int32),
+        ),
+        in_specs=[pl.BlockSpec(memory_space=pl.ANY), pl.BlockSpec(memory_space=pltpu.SMEM)],
+        out_specs=(pl.BlockSpec(memory_space=pl.ANY), pl.BlockSpec(memory_space=pltpu.VMEM),
+                   pl.BlockSpec(memory_space=pltpu.SMEM)),
+        scratch_shapes=[
+            pltpu.VMEM((nd, 8, 128), F32),
+            dma((nd - 1,)), dma((nd - 1,)), dma, dma((nd,)), dma,
+        ],
+        compiler_params=pltpu.CompilerParams(
+            collective_id=1, has_side_effects=True, vmem_limit_bytes=60 * 2 ** 20),
+        name="front",
+    )(tokens, lengths)
 
 
 def per_device(
@@ -519,26 +656,25 @@
     caption_tokens, caption_lengths, group_ids, text_gain, text_gate, text_up, text_down,
     text_proj, image_patches, image_gain, image_fc1, image_fc2, image_proj,
 ):
-    all_lengths = lax.all_gather(caption_lengths, "dp", axis=0, tiled=True)
-    counted = jnp.sum(all_lengths)
-    room = [micro * batch for micro, batch in plans]
-    which = sum((counted > r).astype(jnp.int32) for r in room[:-1])
+    strips, lens, which = front(sizes, plans, caption_tokens, caption_lengths)
     operands = (
-        caption_tokens, all_lengths, group_ids, text_gain, text_gate, text_up, text_down,
+        strips, lens, group_ids, text_gain, text_gate, text_up, text_down,
         text_proj, image_patches, image_gain.reshape(1, -1), image_fc1, image_fc2, image_proj,
     )
-    return lax.switch(which, [functools.partial(towers, sizes, plan) for plan in plans], *operands)
+    branches = [functools.partial(towers, sizes, plan, 2 + i) for i, plan in enumerate(plans)]
+    return lax.switch(which[0, 0], branches, *operands)
 
 
 def towers(
-    sizes, plan,
-    caption_tokens, caption_lengths, group_ids, text_gain, text_gate, text_up, text_down,
+    sizes, plan, barrier_id,
+    strips, caption_lengths, group_ids, text_gain, text_gate, text_up, text_down,
     text_proj, image_patches, image_gain, image_fc1, image_fc2, image_proj,
 ):
     ns, nd, nm = sizes
     grp = nm // nd
     micro, batch = plan
-    caps, slots, piece = caption_tokens.shape
+    _, caps, slots, strip = strips.shape
+    piece = 2 * strip
     length = batch // nd
     ncap = nd * caps
     dl, width = text_gate.shape[1], text_gate.shape[2]
@@ -556,7 +692,7 @@
             jax.ShapeDtypeStruct((caps, embed), F32),
             jax.ShapeDtypeStruct((1, embed), F32),
         ),
-        in_specs=[any_spec, smem, smem, vmem, any_spec, any_spec, any_spec, any_spec,
+        in_specs=[any_spec, vmem, smem, vmem, any_spec, any_spec, any_spec, any_spec,
                   any_spec, vmem, any_spec, any_spec, any_spec],
         out_specs=(vmem, vmem, vmem),
         scratch_shapes=[
@@ -569,16 +705,14 @@
             pltpu.VMEM(image_patches.shape, BF16),
             pltpu.VMEM((nd, caps, slots, piece // 2), BF16),
             pltpu.VMEM((micro, batch, dl), BF16),
-            pltpu.VMEM((batch, dl), BF16),
-            pltpu.VMEM((micro, batch, 2 * width + 128), BF16),
+            pltpu.VMEM((micro, length, 2 * width + 128), BF16),
+            pltpu.VMEM((micro, 3 * length, 2 * width + 128), BF16),
             pltpu.VMEM((micro, length, width), BF16),
             pltpu.VMEM((micro, length, width + 128), BF16),
             pltpu.VMEM((micro, 2, length, 2 * width + 128), BF16),
             pltpu.VMEM((micro, batch, width), BF16),
             pltpu.VMEM((micro, batch, dl), BF16),
-            pltpu.VMEM((micro, nd - 1, length, dl), BF16),
-            pltpu.VMEM((micro, length, dl), BF16),
-            pltpu.VMEM((micro, grp - 1, length, piece), BF16),
+            pltpu.VMEM((micro, nm - 1, length, piece), BF16),
             pltpu.VMEM((micro, length, piece), BF16),
             pltpu.VMEM((nm - 1, dv // 128, 128), F32),
             pltpu.VMEM((dv // 128, 128), F32),
@@ -592,15 +726,15 @@
             pltpu.VMEM((nm - 1, ncap, piece), F32),
             pltpu.VMEM((ncap, embed), BF16),
             pltpu.VMEM((nf - 1, ncap, embed), BF16),
-            pltpu.VMEM((24, embed), F32),
-            dma((8,)), dma, *([dma((micro,))] * 18),
-            dma, dma((micro,)), dma, dma, dma, dma, dma, dma, dma((grp,)), dma, dma, dma, dma((ns * nd,)), dma,
+            pltpu.VMEM((8, embed), F32),
+            dma((9,)), *([dma((micro,))] * 13), dma((nd - 1, micro)),
+            dma((micro,)), dma, dma, dma, dma, dma, dma, dma((grp,)), dma, dma, dma, dma((ns * nd,)), dma,
         ],
         compiler_params=pltpu.CompilerParams(
-            has_side_effects=True, vmem_limit_bytes=60 * 2 ** 20),
+            collective_id=barrier_id, has_side_effects=True, vmem_limit_bytes=60 * 2 ** 20),
         name=f"towers_{micro}_{batch}",
     )(
-        caption_tokens, caption_lengths, group_ids, text_gain, text_gate, text_up, text_down,
+        strips, caption_lengths, group_ids, text_gain, text_gate, text_up, text_down,
         text_proj, image_patches, image_gain, image_fc1, image_fc2, image_proj,
     )
     return loss[0, 0], gcap, gimg

time: 239 us -> 192 us (0.80)
  Pallas kernels: 221 us -> 187 us
  blocking collectives: 7.69 us -> 0 us
    pallas_call x1, Pallas kernels: 221 us -> 179 us  [towers(): pl.pallas_call(functools.partial(kernel, sizes), out_shape=(jax.ShapeDtyp...]
    pallas_call x0 -> x1, Pallas kernels: none -> 8.14 us  [front(): pl.pallas_call(functools.partial(front_kernel, sizes, [micro * batch for...]
    unnamed x1 -> x0, blocking collectives: 7.69 us -> none
where the time goes in v3:
time: 192 us; the launch traced here: 191 us
  Pallas kernels  187 us (97%)
  between operations  2.9 us (2%)
    pallas_call x1, Pallas kernels, towers(): pl.pallas_call(functools.partial(kernel, sizes), out_shape=(jax.ShapeDtyp...  179 us
    pallas_call x1, Pallas kernels, front(): pl.pallas_call(functools.partial(front_kernel, sizes, [micro * batch for...  8.14 us

profile of v3, /device:TPU:1, one launch (start us, length us, event | category | flops | bytes accessed | tf_op | source)
XLA Modules:
  0.0 191.3 jit_solution(13882483801504885726)
XLA Ops:
  0.6 8.1 %front.1 = (bf16[4,4,64,128]{3,2,1,0:T(8,128)(2,1)S(1)}, f32[4,8,128]{2,1,0:T(8,128)S(1)}, s32[1,1]{1,0:T(1,128)}) custom-call(bf16[4,64,256]{2,1,0:T(8,128)(2,1)} %tok_ref.1, s32[4]{0:T(128)} %len_ref.1), custom_call_target="tpu_custom_call" | custom-call | tf_op jit(solution)/shard_map/front/pallas_call | solution.py:634
  9.3 179.0 %conditional.1 = (f32[4,768]{1,0:T(4,128)S(1)}, f32[1,768]{1,0:T(1,128)S(1)}, f32[]{:T(128)}) conditional(s32[]{:T(128)} %bitcast.6, (bf16[4,4,64,128]{3,2,1,0:T(8,128)(2,1)S(1)}, f32[4,8,128]{2,1,0:T(8,128)S(1)}, s32[16]{0:T(128)}, f32[1,4096]{1,0:T(1,128)}, bf16[1,1024,896]{2,1,0:T(8,128)(2,1)}, ...), branch_computations={%region_0.0_spmd, %region_1.0_spmd, %region_2.0_spmd, %region_3.0_... | conditional | bytes 24 | solution.py:665
  9.4 178.6 %towers_4_128.1 = (f32[1,128]{1,0:T(1,128)}, f32[4,768]{1,0:T(4,128)S(1)}, f32[1,768]{1,0:T(1,128)S(1)}) custom-call(bf16[4,4,64,128]{3,2,1,0:T(8,128)(2,1)S(1)} %get-tuple-element.172.tok_ref, f32[4,8,128]{2,1,0:T(8,128)S(1)} %get-tuple-element.173.len_ref, s32[16]{0:T(128)} %get-tuple-element.174.gid_ref, f32[1,4096]{1,0:T(1,128)} %get-tuple-element.175.gain_ref, ...), custom_call_target="tpu_custom_call" | custom-call | tf_op jit(solution)/shard_map/cond/branch_1_fun/towers_4_128/pallas_call | solution.py:688
  189.0 0.6 copy.44
  189.6 0.6 copy.45

commit v4 on v3

--- a/solution.py
+++ b/solution.py
@@ -19,7 +19,7 @@
     patch_ref, vgain_ref, fc1_ref, fc2_ref, iproj_ref,
     loss_ref, gcap_ref, gimg_ref,
     w_gu, w_dn, w_tp, w_f1, w_f2, w_ip, patches,
-    tok_buf, x_buf, far_buf, p_buf, ra_buf, rb_buf, r_buf, i_buf, q_buf, s_buf, h_buf,
+    tok_buf, pos_buf, x_buf, far_buf, p_buf, ra_buf, rb_buf, r_buf, i_buf, q_buf, s_buf, h_buf,
     im1, im1_own, im2, im2_own, imrow, mean_h,
     pin, pin_o, pd, pdr, emb, embr, outb,
     wsem, xr, pa_s, pa_r, pb_s, pb_r, pc_s, pc_r, pd_s2, pd_r2,
@@ -62,56 +62,56 @@
     rows_y = pl.ds(pl.multiple_of(my_group * length, length), length)
     cols_z = pl.ds(pl.multiple_of(my_q * piece, piece), piece)
 
-    root = grp * lax.rem(dp + 1, nd)
-    nf = nd * grp
-    me_f = dp * grp + my_q
-    final_mp = dp * grp + my_q
-    barrier = pltpu.get_barrier_semaphore()
-
-    def hello(where):
-        pl.semaphore_signal(barrier, inc=1, device_id=where, device_id_type=MESH)
-
-    def each(lo, hi, body):
-        def step(o, _):
-            body(o)
-            return 0
-
-        lax.fori_loop(lo, hi, step, 0)
-
-    each(1, nd, lambda o: hello((sec, lax.rem(dp + o, nd), mp)))
-    each(1, nm, lambda o: hello((sec, dp, lax.rem(mp + o, nm))))
-
-    @pl.when(sec > 0)
-    def _():
-        each(0, nm, lambda o: hello((sec - 1, dp, lax.rem(mp + o, nm))))
-
-    @pl.when(is_final)
-    def _():
-        each(0, ns * nd, lambda o: hello((o // nd, lax.rem(o, nd), grp * lax.rem(o + 1, nd))))
-
-        def other_final(o):
-            f = lax.rem(me_f + o, nf)
-            hello((last, f // grp, f))
-
-        each(1, nf, other_final)
-
-    @pl.when(jnp.logical_not(is_final))
-    def _():
-        hello((last, dp, final_mp))
-
     @pl.when(sec == 0)
     def _():
         load(tok_ref, tok_buf, 0)
 
     load(gate_ref.at[0], w_gu.at[:, pl.ds(0, width)], 3)
     load(up_ref.at[0], w_gu.at[:, pl.ds(width, width)], 4)
-
     load(patch_ref, patches, 8)
     load(fc1_ref, w_f1, 1)
     load(fc2_ref, w_f2, 2)
     load(down_ref.at[0], w_dn, 5)
     load(tproj_ref, w_tp, 6)
     load(iproj_ref, w_ip, 7)
+
+    root = grp * lax.rem(dp + 1, nd)
+    nf = nd * grp
+    me_f = dp * grp + my_q
+    final_mp = dp * grp + my_q
+    barrier = pltpu.get_barrier_semaphore()
+
+    def hello(where):
+        pl.semaphore_signal(barrier, inc=1, device_id=where, device_id_type=MESH)
+
+    def each(lo, hi, body):
+        def step(o, _):
+            body(o)
+            return 0
+
+        lax.fori_loop(lo, hi, step, 0)
+
+    each(1, nd, lambda o: hello((sec, lax.rem(dp + o, nd), mp)))
+    each(1, nm, lambda o: hello((sec, dp, lax.rem(mp + o, nm))))
+
+    @pl.when(sec > 0)
+    def _():
+        each(0, nm, lambda o: hello((sec - 1, dp, lax.rem(mp + o, nm))))
+
+    @pl.when(is_final)
+    def _():
+        each(0, ns * nd, lambda o: hello((o // nd, lax.rem(o, nd), grp * lax.rem(o + 1, nd))))
+
+        def other_final(o):
+            f = lax.rem(me_f + o, nf)
+            hello((last, f // grp, f))
+
+        each(1, nf, other_final)
+
+    @pl.when(jnp.logical_not(is_final))
+    def _():
+        hello((last, dp, final_mp))
+
     partners = nd - 1 + nm - 1 + jnp.where(sec < last, nm, 0) + jnp.where(mp == root, nd * grp, 0)
     partners = partners + jnp.where(is_final, nf - 1 + ns * nd - 1, 0)
     pl.semaphore_wait(barrier, partners)
@@ -188,19 +188,25 @@
     full = 2 * width + 128
     low_cols, high_cols = pl.ds(0, width), pl.ds(width, width + 128)
 
+    def ranked(t):
+        y, z = lax.rem(my_group + t // grp + 2, nd), lax.rem(my_q + t + grp // 2, grp)
+        return y * grp + z
+
     def mp_peers(body):
-        def step(o, _):
-            peer = lax.rem(mp + o, nm)
-            body(peer, nm - 1 - o)
-            return 0
-
-        lax.fori_loop(1, nm, step, 0)
+        def one(t):
+            peer = ranked(t)
+
+            @pl.when(peer != mp)
+            def _():
+                body(peer, lax.rem(mp - peer - 1 + 2 * nm, nm))
+
+        each(0, nm, one)
 
     half_rows = pl.ds(pl.multiple_of((my_group // 2) * (batch // 2), batch // 2), batch // 2)
 
     strip_cols = pl.ds(pl.multiple_of(my_q * piece + lax.rem(my_group, 2) * strip, strip), strip)
 
-    def pack():
+    def positions():
         loaded(tok_buf, 0)
         lane = lax.broadcasted_iota(jnp.int32, (8, ncap * slots), 1)
         cap = lane // slots
@@ -208,23 +214,21 @@
         for c in range(ncap):
             at = (lane - c * slots).astype(F32)
             pos = jnp.where(jnp.logical_and(cap == c, at < counts[c]), starts[c] + at, pos)
+        pos_buf[...] = pos
+
+    def pack(b):
+        row = lax.broadcasted_iota(jnp.int32, (batch // 2, ncap * slots), 0)
+        row = (row + (b * batch + (my_group // 2) * (batch // 2))).astype(F32)
+        picks = jnp.where(row == pos_buf[0:1], 1.0, 0.0).astype(BF16)
         tokens = tok_buf[...].reshape(ncap * slots, strip)
-
-        def one(b, _):
-            row = lax.broadcasted_iota(jnp.int32, (batch // 2, ncap * slots), 0)
-            row = (row + (b * batch + (my_group // 2) * (batch // 2))).astype(F32)
-            picks = jnp.where(row == pos[0:1], 1.0, 0.0).astype(BF16)
-            here = x_buf.at[b, half_rows, strip_cols]
-            x_buf[b, half_rows, strip_cols] = jnp.dot(
-                picks, tokens, preferred_element_type=F32).astype(BF16)
-            mp_peers(lambda peer, slot: send(here, here, cs.at[b], xr.at[b], (sec, dp, peer)))
-            return 0
-
-        lax.fori_loop(0, micro, one, 0)
+        here = x_buf.at[b, half_rows, strip_cols]
+        x_buf[b, half_rows, strip_cols] = jnp.dot(picks, tokens, preferred_element_type=F32).astype(BF16)
+        mp_peers(lambda peer, slot: send(here, here, cs.at[b], xr.at[b], (sec, dp, peer)))
 
     @pl.when(sec == 0)
     def _():
-        pack()
+        positions()
+        each(0, min(2, micro), pack)
 
     def products(rows, out):
         x = rows.astype(F32)
@@ -305,7 +309,8 @@
             for at, source in enumerate(sources):
                 q_buf[b, chunk(source), :] = out[at * length:(at + 1) * length]
 
-                def to_owner(z, source=source):
+                def to_owner(o, source=source):
+                    z = lax.rem(my_q + o + grp // 2, grp)
                     owner = source * grp + z
 
                     @pl.when(owner != mp)
@@ -326,12 +331,8 @@
             total = total + s_buf[b, i].astype(F32)
         h_buf[b] = total.astype(BF16)
 
-        def onward(o, _):
-            send(h_buf.at[b], x_buf.at[b, rows_y, cols_z], hs.at[b], xr.at[b],
-                 (sec + 1, dp, lax.rem(mp + o, nm)))
-            return 0
-
-        lax.fori_loop(0, nm, onward, 0)
+        each(0, nm, lambda t: send(
+            h_buf.at[b], x_buf.at[b, rows_y, cols_z], hs.at[b], xr.at[b], (sec + 1, dp, ranked(t))))
 
     def tick(i, _):
         def at(stage, back, also=True):
@@ -347,6 +348,10 @@
         @pl.when(jnp.logical_and(inside, i == 1))
         def _():
             loaded(w_dn, 5)
+
+        @pl.when(jnp.logical_and(sec == 0, i + 2 < micro))
+        def _():
+            pack(i + 2)
 
         at(stage_c, 1, inside)
         at(stage_a2, 0)
@@ -454,8 +459,11 @@
         by_col = jnp.where(by_col > 0, by_col, 1.0)
         good_col = jnp.sum(good, 0, keepdims=True)
         good_col = jnp.where(good_col > 0, good_col, 1.0)
-        forward = jnp.sum(jnp.log(by_row)) - jnp.sum(logits * match * real)
-        backward = jnp.sum(jnp.log(by_col)) - jnp.sum(jnp.log(good_col))
+        def whole(array):
+            return jnp.sum(jnp.sum(array, 0, keepdims=True), 1, keepdims=True)
+
+        forward = whole(jnp.log(by_row)) - whole(logits * match * real)
+        backward = whole(jnp.log(by_col) - jnp.log(good_col))
         loss = 0.5 * (forward / ncap + backward / nd)
         slope = 5.0 * (expo / by_row - match * real + expo / by_col - good / good_col)
         gcap = jnp.zeros(cu.shape, F32)
@@ -468,7 +476,7 @@
             mine = mine + jnp.where(dp == d, 1.0, 0.0) * gcap[caps * d:caps * d + caps]
         outb[0:caps, :] = mine
         outb[caps:caps + 1, :] = gimg
-        outb[caps + 1:8, :] = jnp.full((7 - caps, cu.shape[1]), loss, F32)
+        outb[caps + 1:8, :] = jnp.broadcast_to(loss, (7 - caps, cu.shape[1]))
 
         def fan(t, _):
             s, target, home = fan_target(t)
@@ -704,6 +712,7 @@
             pltpu.VMEM((dv, embed), BF16),
             pltpu.VMEM(image_patches.shape, BF16),
             pltpu.VMEM((nd, caps, slots, piece // 2), BF16),
+            pltpu.VMEM((8, ncap * slots), F32),
             pltpu.VMEM((micro, batch, dl), BF16),
             pltpu.VMEM((micro, length, 2 * width + 128), BF16),
             pltpu.VMEM((micro, 3 * length, 2 * width + 128), BF16),

time: 192 us -> 192 us (level)
  no operation moved by 1% of the time
where the time goes in v4:
time: 192 us
  Pallas kernels  188 us (98%)
  between operations  2.9 us (2%)
    pallas_call x1, Pallas kernels, towers(): pl.pallas_call(functools.partial(kernel, sizes), out_shape=(jax.ShapeDtyp...  179 us
    pallas_call x1, Pallas kernels, front(): pl.pallas_call(functools.partial(front_kernel, sizes, [micro * batch for...  8.14 us

profile of v4, /device:TPU:1, one launch (start us, length us, event | category | flops | bytes accessed | tf_op | source)
XLA Modules:
  0.0 192.2 jit_solution(11556238427394672973)
XLA Ops:
  0.6 8.1 %front.1 = (bf16[4,4,64,128]{3,2,1,0:T(8,128)(2,1)S(1)}, f32[4,8,128]{2,1,0:T(8,128)S(1)}, s32[1,1]{1,0:T(1,128)}) custom-call(bf16[4,64,256]{2,1,0:T(8,128)(2,1)} %tok_ref.1, s32[4]{0:T(128)} %len_ref.1), custom_call_target="tpu_custom_call" | custom-call | tf_op jit(solution)/shard_map/front/pallas_call | solution.py:642
  9.3 180.0 %conditional.1 = (f32[4,768]{1,0:T(4,128)S(1)}, f32[1,768]{1,0:T(1,128)S(1)}, f32[]{:T(128)}) conditional(s32[]{:T(128)} %bitcast.6, (bf16[4,4,64,128]{3,2,1,0:T(8,128)(2,1)S(1)}, f32[4,8,128]{2,1,0:T(8,128)S(1)}, s32[16]{0:T(128)}, f32[1,4096]{1,0:T(1,128)}, bf16[1,1024,896]{2,1,0:T(8,128)(2,1)}, ...), branch_computations={%region_0.0_spmd, %region_1.0_spmd, %region_2.0_spmd, %region_3.0_... | conditional | bytes 24 | solution.py:673
  9.4 179.4 %towers_3_192.1 = (f32[1,128]{1,0:T(1,128)}, f32[4,768]{1,0:T(4,128)S(1)}, f32[1,768]{1,0:T(1,128)S(1)}) custom-call(bf16[4,4,64,128]{3,2,1,0:T(8,128)(2,1)S(1)} %get-tuple-element.188.tok_ref, f32[4,8,128]{2,1,0:T(8,128)S(1)} %get-tuple-element.189.len_ref, s32[16]{0:T(128)} %get-tuple-element.190.gid_ref, f32[1,4096]{1,0:T(1,128)} %get-tuple-element.191.gain_ref, ...), custom_call_target="tpu_custom_call" | custom-call | tf_op jit(solution)/shard_map/cond/branch_2_fun/towers_3_192/pallas_call | solution.py:696
  189.9 0.6 copy.44
  190.5 0.6 copy.45

commit v5 on v4

--- a/solution.py
+++ b/solution.py
@@ -239,7 +239,7 @@
         out[:, pl.ds(0, 2 * width)] = jnp.dot(
             (x * gain).astype(BF16), w_gu[...], preferred_element_type=F32).astype(BF16)
 
-    def stage_a(b):
+    def stage_far(b):
         @pl.when(sec == 0)
         def _():
             drain(s_buf.at[b], xr.at[b])
@@ -251,12 +251,14 @@
         products(x_buf[b, chunk(far), :], far_buf.at[b])
         send(far_buf.at[b, :, low_cols], ra_buf.at[b], pa_s.at[b], pa_r.at[b], (sec, right, mp))
         send(far_buf.at[b, :, high_cols], rb_buf.at[b], pb_s.at[b], pb_r.at[b], (sec, left, mp))
+
+    def stage_near(b):
         near = jnp.concatenate([x_buf[b, chunk(c), :] for c in (right, left, dp)], 0)
         products(near, p_buf.at[b])
 
     to_right, to_left, to_self = pl.ds(0, length), pl.ds(length, length), pl.ds(2 * length, length)
 
-    def stage_a2(b):
+    def stage_relay(b):
         drain(ra_buf.at[b], pa_r.at[b])
         p_buf[b, to_right, low_cols] = (
             p_buf[b, to_right, low_cols].astype(F32) + ra_buf[b].astype(F32)).astype(BF16)
@@ -298,31 +300,33 @@
                 mean_h[...] = mean_h[...] + jnp.dot(
                     members(b * batch, batch), x_buf[b, :, cols_z], preferred_element_type=F32)
 
-    def stage_c(b):
-        def from_sources(offsets):
-            sources = [lax.rem(dp + o, nd) for o in offsets]
-            for o, source in zip(offsets, sources):
-                if o:
-                    drain(i_buf.at[b, chunk(source)], ir.at[o - 1, b])
-            out = jnp.dot(jnp.concatenate([i_buf[b, chunk(c), :] for c in sources], 0), w_dn[...],
-                          preferred_element_type=F32).astype(BF16)
-            for at, source in enumerate(sources):
-                q_buf[b, chunk(source), :] = out[at * length:(at + 1) * length]
-
-                def to_owner(o, source=source):
-                    z = lax.rem(my_q + o + grp // 2, grp)
-                    owner = source * grp + z
-
-                    @pl.when(owner != mp)
-                    def _():
-                        slot = lax.rem(mp - owner - 1 + 2 * nm, nm)
-                        send(q_buf.at[b, chunk(source), pl.ds(pl.multiple_of(z * piece, piece), piece)],
-                             s_buf.at[b, slot], qs.at[b], qr.at[b], (sec, dp, owner))
-
-                each(0, grp, to_owner)
-
-        from_sources((0, 1, nd - 1))
-        from_sources((2,))
+    def down(b, offsets):
+        sources = [lax.rem(dp + o, nd) for o in offsets]
+        for o, source in zip(offsets, sources):
+            if o:
+                drain(i_buf.at[b, chunk(source)], ir.at[o - 1, b])
+        out = jnp.dot(jnp.concatenate([i_buf[b, chunk(c), :] for c in sources], 0), w_dn[...],
+                      preferred_element_type=F32).astype(BF16)
+        for at, source in enumerate(sources):
+            q_buf[b, chunk(source), :] = out[at * length:(at + 1) * length]
+
+            def to_owner(o, source=source):
+                z = lax.rem(my_q + o + grp // 2, grp)
+                owner = source * grp + z
+
+                @pl.when(owner != mp)
+                def _():
+                    slot = lax.rem(mp - owner - 1 + 2 * nm, nm)
+                    send(q_buf.at[b, chunk(source), pl.ds(pl.multiple_of(z * piece, piece), piece)],
+                         s_buf.at[b, slot], qs.at[b], qr.at[b], (sec, dp, owner))
+
+            each(0, grp, to_owner)
+
+    def stage_down_near(b):
+        down(b, (0, 1, nd - 1))
+
+    def stage_down_far(b):
+        down(b, (2,))
 
     def stage_d(b):
         drain(s_buf.at[b], qr.at[b])
@@ -341,20 +345,23 @@
                 stage(i - back)
 
         inside = sec < last
+        at(stage_far, 0)
+        at(stage_b, 1)
+        at(stage_near, 0)
+
+        @pl.when(jnp.logical_and(sec == 0, i + 2 < micro))
+        def _():
+            pack(i + 2)
+
+        at(stage_relay, 0)
+
+        @pl.when(jnp.logical_and(inside, i == 1))
+        def _():
+            loaded(w_dn, 5)
+
+        at(stage_down_near, 1, inside)
         at(stage_d, 2, inside)
-        at(stage_b, 1)
-        at(stage_a, 0)
-
-        @pl.when(jnp.logical_and(inside, i == 1))
-        def _():
-            loaded(w_dn, 5)
-
-        @pl.when(jnp.logical_and(sec == 0, i + 2 < micro))
-        def _():
-            pack(i + 2)
-
-        at(stage_c, 1, inside)
-        at(stage_a2, 0)
+        at(stage_down_far, 1, inside)
         return 0
 
     lax.fori_loop(0, micro + 2, tick, 0)

time: 192 us -> 187 us (0.974)
  Pallas kernels: 188 us -> 184 us
    pallas_call x1, Pallas kernels: 179 us -> 176 us  [towers(): pl.pallas_call(functools.partial(kernel, sizes), out_shape=(jax.ShapeDtyp...]
where the time goes in v5:
time: 187 us; the launch traced here: 189 us
  Pallas kernels  184 us (98%)
  between operations  2.9 us (2%)
    pallas_call x1, Pallas kernels, towers(): pl.pallas_call(functools.partial(kernel, sizes), out_shape=(jax.ShapeDtyp...  176 us
    pallas_call x1, Pallas kernels, front(): pl.pallas_call(functools.partial(front_kernel, sizes, [micro * batch for...  8.14 us

profile of v5, /device:TPU:1, one launch (start us, length us, event | category | flops | bytes accessed | tf_op | source)
XLA Modules:
  0.0 188.9 jit_solution(5593878532554290946)
XLA Ops:
  0.6 8.1 %front.1 = (bf16[4,4,64,128]{3,2,1,0:T(8,128)(2,1)S(1)}, f32[4,8,128]{2,1,0:T(8,128)S(1)}, s32[1,1]{1,0:T(1,128)}) custom-call(bf16[4,64,256]{2,1,0:T(8,128)(2,1)} %tok_ref.1, s32[4]{0:T(128)} %len_ref.1), custom_call_target="tpu_custom_call" | custom-call | tf_op jit(solution)/shard_map/front/pallas_call | solution.py:649
  9.3 176.7 %conditional.1 = (f32[4,768]{1,0:T(4,128)S(1)}, f32[1,768]{1,0:T(1,128)S(1)}, f32[]{:T(128)}) conditional(s32[]{:T(128)} %bitcast.6, (bf16[4,4,64,128]{3,2,1,0:T(8,128)(2,1)S(1)}, f32[4,8,128]{2,1,0:T(8,128)S(1)}, s32[16]{0:T(128)}, f32[1,4096]{1,0:T(1,128)}, bf16[1,1024,896]{2,1,0:T(8,128)(2,1)}, ...), branch_computations={%region_0.0_spmd, %region_1.0_spmd, %region_2.0_spmd, %region_3.0_... | conditional | bytes 24 | solution.py:680
  9.5 176.2 %towers_5_128.1 = (f32[1,128]{1,0:T(1,128)}, f32[4,768]{1,0:T(4,128)S(1)}, f32[1,768]{1,0:T(1,128)S(1)}) custom-call(bf16[4,4,64,128]{3,2,1,0:T(8,128)(2,1)S(1)} %get-tuple-element.204.tok_ref, f32[4,8,128]{2,1,0:T(8,128)S(1)} %get-tuple-element.205.len_ref, s32[16]{0:T(128)} %get-tuple-element.206.gid_ref, f32[1,4096]{1,0:T(1,128)} %get-tuple-element.207.gain_ref, ...), custom_call_target="tpu_custom_call" | custom-call | tf_op jit(solution)/shard_map/cond/branch_3_fun/towers_5_128/pallas_call | solution.py:703
  186.6 0.6 copy.44
  187.2 0.6 copy.45

commit v6 on v5

--- a/solution.py
+++ b/solution.py
@@ -8,7 +8,7 @@
 from jax.sharding import PartitionSpec as P
 
 MESH = pl.DeviceIdType.MESH
-PLANS = ((3, 128), (4, 128), (3, 192), (5, 128), (4, 192), (4, 256))
+PLANS = ((3, 128), (3, 192), (3, 256), (4, 256))
 BF16 = jnp.bfloat16
 F32 = jnp.float32
 
@@ -89,7 +89,7 @@
             body(o)
             return 0
 
-        lax.fori_loop(lo, hi, step, 0)
+        lax.fori_loop(lo, hi, step, 0, unroll=True)
 
     each(1, nd, lambda o: hello((sec, lax.rem(dp + o, nd), mp)))
     each(1, nm, lambda o: hello((sec, dp, lax.rem(mp + o, nm))))
@@ -195,12 +195,11 @@
     def mp_peers(body):
         def one(t):
             peer = ranked(t)
-
-            @pl.when(peer != mp)
-            def _():
-                body(peer, lax.rem(mp - peer - 1 + 2 * nm, nm))
-
-        each(0, nm, one)
+            body(peer, lax.rem(mp - peer - 1 + 2 * nm, nm))
+
+        itself = (nd - 2) * grp + grp // 2
+        each(0, itself, one)
+        each(itself + 1, nm, one)
 
     half_rows = pl.ds(pl.multiple_of((my_group // 2) * (batch // 2), batch // 2), batch // 2)
 
@@ -228,16 +227,24 @@
     @pl.when(sec == 0)
     def _():
         positions()
-        each(0, min(2, micro), pack)
-
-    def products(rows, out):
+        lax.fori_loop(0, min(2, micro), lambda b, _: (pack(b), 0)[1], 0)
+
+    def products(rows, out, first_done=None):
         x = rows.astype(F32)
+        scaled = (x * gain).astype(BF16)
+        if first_done is None:
+            out[:, pl.ds(0, 2 * width)] = jnp.dot(
+                scaled, w_gu[...], preferred_element_type=F32).astype(BF16)
+        else:
+            out[:, pl.ds(0, width)] = jnp.dot(
+                scaled, w_gu[:, 0:width], preferred_element_type=F32).astype(BF16)
+            first_done()
+            out[:, pl.ds(width, width)] = jnp.dot(
+                scaled, w_gu[:, width:2 * width], preferred_element_type=F32).astype(BF16)
         total = jnp.sum(x * x, -1, keepdims=True)
         high = total.astype(BF16).astype(F32)
         lane = lax.broadcasted_iota(jnp.int32, (x.shape[0], 128), 1)
         out[:, pl.ds(2 * width, 128)] = jnp.where(lane < 64, high, total - high).astype(BF16)
-        out[:, pl.ds(0, 2 * width)] = jnp.dot(
-            (x * gain).astype(BF16), w_gu[...], preferred_element_type=F32).astype(BF16)
 
     def stage_far(b):
         @pl.when(sec == 0)
@@ -248,8 +255,8 @@
         def _():
             drain(x_buf.at[b], xr.at[b])
 
-        products(x_buf[b, chunk(far), :], far_buf.at[b])
-        send(far_buf.at[b, :, low_cols], ra_buf.at[b], pa_s.at[b], pa_r.at[b], (sec, right, mp))
+        products(x_buf[b, chunk(far), :], far_buf.at[b], lambda: send(
+            far_buf.at[b, :, low_cols], ra_buf.at[b], pa_s.at[b], pa_r.at[b], (sec, right, mp)))
         send(far_buf.at[b, :, high_cols], rb_buf.at[b], pb_s.at[b], pb_r.at[b], (sec, left, mp))
 
     def stage_near(b):

time: 187 us -> 203 us (1.086); the launches traced: 189 us -> 203 us
  Pallas kernels: 184 us -> 198 us
    pallas_call x1, Pallas kernels: 176 us -> 190 us  [towers(): pl.pallas_call(functools.partial(kernel, sizes), out_shape=(jax.ShapeDtyp...]
where the time goes in v6:
time: 203 us
  Pallas kernels  198 us (98%)
  between operations  3.03 us (1%)
    pallas_call x1, Pallas kernels, towers(): pl.pallas_call(functools.partial(kernel, sizes), out_shape=(jax.ShapeDtyp...  190 us
    pallas_call x1, Pallas kernels, front(): pl.pallas_call(functools.partial(front_kernel, sizes, [micro * batch for...  8.14 us

profile of v6, /device:TPU:1, one launch (start us, length us, event | category | flops | bytes accessed | tf_op | source)
XLA Modules:
  0.0 202.6 jit_solution(4266618108553551083)
XLA Ops:
  0.6 8.1 %front.1 = (bf16[4,4,64,128]{3,2,1,0:T(8,128)(2,1)S(1)}, f32[4,8,128]{2,1,0:T(8,128)S(1)}, s32[1,1]{1,0:T(1,128)}) custom-call(bf16[4,64,256]{2,1,0:T(8,128)(2,1)} %tok_ref.1, s32[4]{0:T(128)} %len_ref.1), custom_call_target="tpu_custom_call" | custom-call | tf_op jit(solution)/shard_map/front/pallas_call | solution.py:656
  9.4 190.2 %conditional.1 = (f32[4,768]{1,0:T(4,128)S(1)}, f32[1,768]{1,0:T(1,128)S(1)}, f32[]{:T(128)}) conditional(s32[]{:T(128)} %bitcast.4, (bf16[4,4,64,128]{3,2,1,0:T(8,128)(2,1)S(1)}, f32[4,8,128]{2,1,0:T(8,128)S(1)}, s32[16]{0:T(128)}, f32[1,4096]{1,0:T(1,128)}, bf16[1,1024,896]{2,1,0:T(8,128)(2,1)}, ...), branch_computations={%region_0.0_spmd, %region_1.0_spmd, %region_2.0_spmd, %region_3.0_... | conditional | bytes 24 | solution.py:687
  9.4 189.7 %towers_3_256.1 = (f32[1,128]{1,0:T(1,128)}, f32[4,768]{1,0:T(4,128)S(1)}, f32[1,768]{1,0:T(1,128)S(1)}) custom-call(bf16[4,4,64,128]{3,2,1,0:T(8,128)(2,1)S(1)} %get-tuple-element.136.tok_ref, f32[4,8,128]{2,1,0:T(8,128)S(1)} %get-tuple-element.137.len_ref, s32[16]{0:T(128)} %get-tuple-element.138.gid_ref, f32[1,4096]{1,0:T(1,128)} %get-tuple-element.139.gain_ref, ...), custom_call_target="tpu_custom_call" | custom-call | tf_op jit(solution)/shard_map/cond/branch_2_fun/towers_3_256/pallas_call | solution.py:710
  200.3 0.6 copy.36
  200.9 0.6 copy.37

commit v7 on v6

--- a/solution.py
+++ b/solution.py
@@ -8,7 +8,7 @@
 from jax.sharding import PartitionSpec as P
 
 MESH = pl.DeviceIdType.MESH
-PLANS = ((3, 128), (3, 192), (3, 256), (4, 256))
+PLANS = ((3, 128), (4, 128), (3, 192), (5, 128), (4, 192), (4, 256))
 BF16 = jnp.bfloat16
 F32 = jnp.float32
 
@@ -112,10 +112,6 @@
     def _():
         hello((last, dp, final_mp))
 
-    partners = nd - 1 + nm - 1 + jnp.where(sec < last, nm, 0) + jnp.where(mp == root, nd * grp, 0)
-    partners = partners + jnp.where(is_final, nf - 1 + ns * nd - 1, 0)
-    pl.semaphore_wait(barrier, partners)
-
     counts = [len_ref[c // caps, c % caps:c % caps + 1, 0:1] for c in range(ncap)]
     starts = [jnp.zeros((1, 1), F32)]
     for c in range(ncap):
@@ -128,6 +124,59 @@
             return 0
 
         lax.fori_loop(1, nd, step, 0)
+
+    def ranked(t):
+        y, z = lax.rem(my_group + t // grp + 2, nd), lax.rem(my_q + t + grp // 2, grp)
+        return y * grp + z
+
+    def mp_peers(body):
+        def one(t):
+            peer = ranked(t)
+            body(peer, lax.rem(mp - peer - 1 + 2 * nm, nm))
+
+        itself = (nd - 2) * grp + grp // 2
+        each(0, itself, one)
+        each(itself + 1, nm, one)
+
+    half_rows = pl.ds(pl.multiple_of((my_group // 2) * (batch // 2), batch // 2), batch // 2)
+
+    strip_cols = pl.ds(pl.multiple_of(my_q * piece + lax.rem(my_group, 2) * strip, strip), strip)
+
+    def positions():
+        loaded(tok_buf, 0)
+        lane = lax.broadcasted_iota(jnp.int32, (8, ncap * slots), 1)
+        cap = lane // slots
+        pos = jnp.full((8, ncap * slots), -1.0, F32)
+        for c in range(ncap):
+            at = (lane - c * slots).astype(F32)
+            pos = jnp.where(jnp.logical_and(cap == c, at < counts[c]), starts[c] + at, pos)
+        pos_buf[...] = pos
+
+    def pack_rows(b):
+        row = lax.broadcasted_iota(jnp.int32, (batch // 2, ncap * slots), 0)
+        row = (row + (b * batch + (my_group // 2) * (batch // 2))).astype(F32)
+        picks = jnp.where(row == pos_buf[0:1], 1.0, 0.0).astype(BF16)
+        tokens = tok_buf[...].reshape(ncap * slots, strip)
+        x_buf[b, half_rows, strip_cols] = jnp.dot(picks, tokens, preferred_element_type=F32).astype(BF16)
+
+    def pack_send(b):
+        here = x_buf.at[b, half_rows, strip_cols]
+        mp_peers(lambda peer, slot: send(here, here, cs.at[b], xr.at[b], (sec, dp, peer)))
+
+    ahead = min(2, micro)
+
+    @pl.when(sec == 0)
+    def _():
+        positions()
+        lax.fori_loop(0, ahead, lambda b, _: (pack_rows(b), 0)[1], 0)
+
+    partners = nd - 1 + nm - 1 + jnp.where(sec < last, nm, 0) + jnp.where(mp == root, nd * grp, 0)
+    partners = partners + jnp.where(is_final, nf - 1 + ns * nd - 1, 0)
+    pl.semaphore_wait(barrier, partners)
+
+    @pl.when(sec == 0)
+    def _():
+        lax.fori_loop(0, ahead, lambda b, _: (pack_send(b), 0)[1], 0)
 
     vtiles = w_f2.shape[1] // 128
 
@@ -188,47 +237,6 @@
     full = 2 * width + 128
     low_cols, high_cols = pl.ds(0, width), pl.ds(width, width + 128)
 
-    def ranked(t):
-        y, z = lax.rem(my_group + t // grp + 2, nd), lax.rem(my_q + t + grp // 2, grp)
-        return y * grp + z
-
-    def mp_peers(body):
-        def one(t):
-            peer = ranked(t)
-            body(peer, lax.rem(mp - peer - 1 + 2 * nm, nm))
-
-        itself = (nd - 2) * grp + grp // 2
-        each(0, itself, one)
-        each(itself + 1, nm, one)
-
-    half_rows = pl.ds(pl.multiple_of((my_group // 2) * (batch // 2), batch // 2), batch // 2)
-
-    strip_cols = pl.ds(pl.multiple_of(my_q * piece + lax.rem(my_group, 2) * strip, strip), strip)
-
-    def positions():
-        loaded(tok_buf, 0)
-        lane = lax.broadcasted_iota(jnp.int32, (8, ncap * slots), 1)
-        cap = lane // slots
-        pos = jnp.full((8, ncap * slots), -1.0, F32)
-        for c in range(ncap):
-            at = (lane - c * slots).astype(F32)
-            pos = jnp.where(jnp.logical_and(cap == c, at < counts[c]), starts[c] + at, pos)
-        pos_buf[...] = pos
-
-    def pack(b):
-        row = lax.broadcasted_iota(jnp.int32, (batch // 2, ncap * slots), 0)
-        row = (row + (b * batch + (my_group // 2) * (batch // 2))).astype(F32)
-        picks = jnp.where(row == pos_buf[0:1], 1.0, 0.0).astype(BF16)
-        tokens = tok_buf[...].reshape(ncap * slots, strip)
-        here = x_buf.at[b, half_rows, strip_cols]
-        x_buf[b, half_rows, strip_cols] = jnp.dot(picks, tokens, preferred_element_type=F32).astype(BF16)
-        mp_peers(lambda peer, slot: send(here, here, cs.at[b], xr.at[b], (sec, dp, peer)))
-
-    @pl.when(sec == 0)
-    def _():
-        positions()
-        lax.fori_loop(0, min(2, micro), lambda b, _: (pack(b), 0)[1], 0)
-
     def products(rows, out, first_done=None):
         x = rows.astype(F32)
         scaled = (x * gain).astype(BF16)
@@ -358,7 +366,8 @@
 
         @pl.when(jnp.logical_and(sec == 0, i + 2 < micro))
         def _():
-            pack(i + 2)
+            pack_rows(i + 2)
+            pack_send(i + 2)
 
         at(stage_relay, 0)
 
@@ -502,14 +511,6 @@
 
         lax.fori_loop(0, ns * nd, fan, 0)
 
-    @pl.when(jnp.logical_not(is_final))
-    def _():
-        drain(outb, out_r)
-
-    loss_ref[...] = outb[caps + 1:caps + 2, 0:128]
-    gcap_ref[...] = outb[0:caps, :]
-    gimg_ref[...] = outb[caps:caps + 1, :]
-
     @pl.when(mp != root)
     def _():
         drain(im1_own, im1_s)
@@ -548,6 +549,14 @@
             return 0
 
         lax.fori_loop(0, grp, sent_pd, 0)
+
+    @pl.when(jnp.logical_not(is_final))
+    def _():
+        drain(outb, out_r)
+
+    loss_ref[...] = outb[caps + 1:caps + 2, 0:128]
+    gcap_ref[...] = outb[0:caps, :]
+    gimg_ref[...] = outb[caps:caps + 1, :]
 
     @pl.when(is_final)
     def _():

time: 203 us -> 183 us (0.901)
  Pallas kernels: 198 us -> 178 us
    pallas_call x1, Pallas kernels: 190 us -> 170 us  [towers(): pl.pallas_call(functools.partial(kernel, sizes), out_shape=(jax.ShapeDtyp...]
where the time goes in v7:
time: 183 us
  Pallas kernels  178 us (97%)
  between operations  2.9 us (2%)
    pallas_call x1, Pallas kernels, towers(): pl.pallas_call(functools.partial(kernel, sizes), out_shape=(jax.ShapeDtyp...  170 us
    pallas_call x1, Pallas kernels, front(): pl.pallas_call(functools.partial(front_kernel, sizes, [micro * batch for...  8.14 us

profile of v7, /device:TPU:1, one launch (start us, length us, event | category | flops | bytes accessed | tf_op | source)
XLA Modules:
  0.0 183.1 jit_solution(4148792749687228367)
XLA Ops:
  0.6 8.1 %front.1 = (bf16[4,4,64,128]{3,2,1,0:T(8,128)(2,1)S(1)}, f32[4,8,128]{2,1,0:T(8,128)S(1)}, s32[1,1]{1,0:T(1,128)}) custom-call(bf16[4,64,256]{2,1,0:T(8,128)(2,1)} %tok_ref.1, s32[4]{0:T(128)} %len_ref.1), custom_call_target="tpu_custom_call" | custom-call | tf_op jit(solution)/shard_map/front/pallas_call | solution.py:665
  9.3 170.9 %conditional.1 = (f32[4,768]{1,0:T(4,128)S(1)}, f32[1,768]{1,0:T(1,128)S(1)}, f32[]{:T(128)}) conditional(s32[]{:T(128)} %bitcast.6, (bf16[4,4,64,128]{3,2,1,0:T(8,128)(2,1)S(1)}, f32[4,8,128]{2,1,0:T(8,128)S(1)}, s32[16]{0:T(128)}, f32[1,4096]{1,0:T(1,128)}, bf16[1,1024,896]{2,1,0:T(8,128)(2,1)}, ...), branch_computations={%region_0.0_spmd, %region_1.0_spmd, %region_2.0_spmd, %region_3.0_... | conditional | bytes 24 | solution.py:696
  9.4 170.3 %towers_3_192.1 = (f32[1,128]{1,0:T(1,128)}, f32[4,768]{1,0:T(4,128)S(1)}, f32[1,768]{1,0:T(1,128)S(1)}) custom-call(bf16[4,4,64,128]{3,2,1,0:T(8,128)(2,1)S(1)} %get-tuple-element.188.tok_ref, f32[4,8,128]{2,1,0:T(8,128)S(1)} %get-tuple-element.189.len_ref, s32[16]{0:T(128)} %get-tuple-element.190.gid_ref, f32[1,4096]{1,0:T(1,128)} %get-tuple-element.191.gain_ref, ...), custom_call_target="tpu_custom_call" | custom-call | tf_op jit(solution)/shard_map/cond/branch_2_fun/towers_3_192/pallas_call | solution.py:719
  180.8 0.6 copy.44
  181.4 0.6 copy.45
